TPU v7x, 128 devices: a whole 4x4x4 slice. The times are simulated.
128 devices in a mesh: grp: 8 (over x_lo, y), shard: 16 (over x_hi, z, core).
Axes of the slice: x: 4 (x_hi: 2, x_lo: 2; x = x_hi * 2 + x_lo), y: 4, z: 4, core: 2. Of those that a mesh axis runs over, the one named last changes fastest.
Arguments:
- tokens: bfloat16 [2048, 4096], P('grp'), may hold values from -6 to 6
- gate_weight: bfloat16 [4096, 14336], P('grp', 'shard'), may hold values from -0.09375 to 0.09375
- up_weight: bfloat16 [4096, 14336], P('grp', 'shard'), may hold values from -0.09375 to 0.09375
- down_weight: bfloat16 [14336, 4096], P('shard', 'grp'), may hold values from -0.046875 to 0.046875
- grad_out: bfloat16 [2048, 4096], P('grp'), may hold values from -6 to 6
Outputs:
- grad_tokens: bfloat16 [2048, 4096], P('shard', 'grp')
- grad_gate: float32 [4096, 14336], P('grp', 'shard')
- grad_up: float32 [4096, 14336], P('grp', 'shard')
- grad_down: float32 [14336, 4096], P('shard', 'grp')
All inputs are finite; a program needn't handle non-finite values.
Results may differ from a plain program's by a relative error of at most 0.013.
Values may be sent and summed in bfloat16 or wider, within the bound.
A program may use at most 128 MiB of HBM per device.

v0:
```python
import jax
import jax.numpy as jnp
from jax import lax
from jax.sharding import PartitionSpec as P


def contract_rows(left, right):
    return lax.dot_general(
        left, right, (((0,), (0,)), ((), ())), preferred_element_type=jnp.float32
    )


def contract_cols(left, right):
    return lax.dot_general(
        left, right, (((1,), (1,)), ((), ())), preferred_element_type=jnp.float32
    )


def local(tokens, gate_weight, up_weight, down_weight, grad_out):
    groups = lax.axis_size("grp")
    row_count = tokens.shape[0]
    model_width = tokens.shape[1]
    col_block = model_width // groups
    token_split = tokens.reshape(row_count, groups, col_block)
    grad_split = grad_out.reshape(row_count, groups, col_block)
    token_blocks, grad_blocks = (
        lax.all_to_all(token_split, "grp", split_axis=1, concat_axis=0, tiled=True),
        lax.all_to_all(grad_split, "grp", split_axis=1, concat_axis=0, tiled=True),
    )
    grad_blocks = grad_blocks.reshape(groups * row_count, col_block)
    token_blocks = token_blocks.reshape(groups * row_count, col_block)
    gate_add = jnp.dot(
        tokens,
        lax.all_gather(gate_weight, "grp", axis=0, tiled=True),
        preferred_element_type=jnp.float32,
    )
    up_add = jnp.dot(
        tokens,
        lax.all_gather(up_weight, "grp", axis=0, tiled=True),
        preferred_element_type=jnp.float32,
    )
    gate_sigmoid = jax.nn.sigmoid(gate_add)
    silu_gate = gate_add * gate_sigmoid
    hidden = (silu_gate * up_add).astype(jnp.bfloat16)
    back_grad = contract_cols(grad_out, lax.all_gather(down_weight, "grp", axis=1, tiled=True))
    delta_gate = (
        back_grad * up_add * gate_sigmoid * (1.0 + gate_add * (1.0 - gate_sigmoid))
    ).astype(jnp.bfloat16)
    delta_up = (back_grad * silu_gate).astype(jnp.bfloat16)
    all_hidden, all_delta_gate, all_delta_up = (
        lax.all_gather(hidden, "grp", axis=0, tiled=True),
        lax.all_gather(delta_gate, "grp", axis=0, tiled=True),
        lax.all_gather(delta_up, "grp", axis=0, tiled=True),
    )
    grad_down = contract_rows(all_hidden, grad_blocks)
    grad_tokens = lax.psum_scatter(
        contract_cols(all_delta_gate, gate_weight) + contract_cols(all_delta_up, up_weight),
        "shard",
        scatter_dimension=0,
        tiled=True,
    ).astype(jnp.bfloat16)
    grad_gate = contract_rows(token_blocks, all_delta_gate)
    grad_up = contract_rows(token_blocks, all_delta_up)
    return (grad_tokens, grad_gate, grad_up, grad_down)


def solution(mesh):
    return jax.shard_map(
        local,
        mesh=mesh,
        in_specs=(
            P("grp", None),
            P("grp", "shard"),
            P("grp", "shard"),
            P("shard", "grp"),
            P("grp", None),
        ),
        out_specs=(P("shard", "grp"), P("grp", "shard"), P("grp", "shard"), P("shard", "grp")),
        check_vma=False,
    )
```

profile of v0, /device:TPU:0, one launch (start us, length us, event | category | flops | bytes accessed | tf_op | source)
XLA Modules:
  0.0 542.5 jit_solution(7873023626449861885)
XLA Ops:
  7.2 0.0 all-gather.7.cloned.1.call-start
  7.2 0.7 all-gather.7.cloned.1.call-update
  7.9 0.0 all-gather.11.cloned.1.call-start
  7.9 0.7 all-gather.11.cloned.1.call-update
  8.6 0.0 all-gather.9.cloned.1.call-start
  8.7 0.7 all-gather.9.cloned.1.call-update
  9.4 0.0 copy-start.2
  9.4 0.0 all-gather.13.cloned.1.call-start
  9.4 84.8 %all-gather.7.cloned.1.call-done = bf16[896,4096]{1,0:T(8,128)(2,1)} async-done(((bf16[896,512]{1,0:T(8,128)(2,1)}), bf16[896,4096]{1,0:T(8,128)(2,1)}) %all-gather.7.cloned.1.call-update) | async-done | bytes 7340048 | tf_op jit(solution)/shard_map/all_gather | solution.py:45
  94.2 7.0 %fusion.1 = f32[256,896]{1,0:T(8,128)} fusion(bf16[256,4096]{1,0:T(8,128)(2,1)} %param.9, bf16[896,4096]{1,0:T(8,128)(2,1)} %all-gather.7.cloned.1.call-done), kind=kOutput, calls=%fused_computation.8 | convolution fusion | flops 1879048192 | bytes 10354688 | tf_op jit(solution)/shard_map/dot_general | solution.py:14
  101.2 75.5 %all-gather.11.cloned.1.call-done = bf16[4096,896]{1,0:T(8,128)(2,1)} async-done(((bf16[512,896]{1,0:T(8,128)(2,1)}), bf16[4096,896]{1,0:T(8,128)(2,1)}) %all-gather.11.cloned.1.call-update) | async-done | bytes 7340048 | tf_op jit(solution)/shard_map/all_gather | solution.py:34
  176.8 0.0 copy-done.2
  176.8 6.3 %fusion.2 = f32[256,896]{1,0:T(8,128)} fusion(bf16[256,4096]{1,0:T(8,128)(2,1)S(1)} %copy-done.2, bf16[4096,896]{1,0:T(8,128)(2,1)} %all-gather.11.cloned.1.call-done), kind=kOutput, calls=%fused_computation.9 | convolution fusion | flops 1879048192 | bytes 10354688 | tf_op jit(solution)/shard_map/dot_general | solution.py:32
  183.1 0.0 copy-start.3
  183.1 76.2 %all-gather.9.cloned.1.call-done = bf16[4096,896]{1,0:T(8,128)(2,1)} async-done(((bf16[512,896]{1,0:T(8,128)(2,1)}), bf16[4096,896]{1,0:T(8,128)(2,1)}) %all-gather.9.cloned.1.call-update) | async-done | bytes 7340048 | tf_op jit(solution)/shard_map/all_gather | solution.py:39
  259.3 7.2 %multiply_convert_fusion = (bf16[256,896]{1,0:T(8,128)(2,1)}, bf16[256,896]{1,0:T(8,128)(2,1)}, bf16[256,896]{1,0:T(8,128)(2,1)}) fusion(f32[256,896]{1,0:T(8,128)} %fusion.2, f32[256,896]{1,0:T(8,128)} %fusion.1, bf16[256,4096]{1,0:T(8,128)(2,1)S(1)} %copy-done.2, bf16[4096,896]{1,0:T(8,128)(2,1)} %all-gather.9.cloned.1.call-done), kind=kOutput, calls=%fused_computation.3 | convolution fusion | flops 1882488832 | bytes 12648448 | tf_op jit(solution)/shard_map/dot_general | solution.py:37
  266.5 0.0 all-gather.13.cloned.1.call-update
  266.5 0.0 all-gather.15.cloned.1.call-start
  266.6 0.5 all-gather.15.cloned.1.call-update
  267.1 0.0 all-gather.17.cloned.1.call-start
  267.2 0.5 all-gather.17.cloned.1.call-update
  267.7 0.0 reduce-scatter.2.cloned.1.call-start
  267.7 45.4 %all-gather.13.cloned.1.call-done = bf16[2048,896]{1,0:T(8,128)(2,1)} async-done(((bf16[256,896]{1,0:T(8,128)(2,1)}), bf16[2048,896]{1,0:T(8,128)(2,1)}) %all-gather.13.cloned.1.call-update) | async-done | bytes 3670032 | tf_op jit(solution)/shard_map/all_gather | solution.py:52
  313.1 0.0 copy-done.3
  313.1 6.4 %fusion.3 = f32[2048,512]{1,0:T(8,128)} fusion(bf16[2048,896]{1,0:T(8,128)(2,1)} %all-gather.13.cloned.1.call-done, bf16[512,896]{1,0:T(8,128)(2,1)S(1)} %copy-done.3), kind=kOutput, calls=%fused_computation.10 | convolution fusion | flops 1879048192 | bytes 8781824 | tf_op jit(solution)/shard_map/dot_general | solution.py:14
  319.5 42.1 %all-gather.15.cloned.1.call-done = bf16[2048,896]{1,0:T(8,128)(2,1)} async-done(((bf16[256,896]{1,0:T(8,128)(2,1)}), bf16[2048,896]{1,0:T(8,128)(2,1)}) %all-gather.15.cloned.1.call-update) | async-done | bytes 3670032 | tf_op jit(solution)/shard_map/all_gather | solution.py:53
  361.6 7.9 %convolution_add_fusion = f32[2048,512]{1,0:T(8,128)} fusion(f32[2048,512]{1,0:T(8,128)} %fusion.3, bf16[2048,896]{1,0:T(8,128)(2,1)} %all-gather.15.cloned.1.call-done, bf16[512,896]{1,0:T(8,128)(2,1)} %param.7), kind=kOutput, calls=%fused_computation | convolution fusion | flops 1880096768 | bytes 12976128 | tf_op jit(solution)/shard_map/dot_general | solution.py:14
  369.5 0.0 reduce-scatter.2.cloned.1.call-update
  369.6 2.5 copy.13
  372.1 3.6 all-to-all-start
  375.7 4.1 copy.15
  379.8 45.2 %all-to-all-done = bf16[256,8,512]{0,2,1:T(8,128)(2,1)S(1)} async-done(((bf16[256,8,512]{0,2,1:T(8,128)(2,1)}), bf16[256,8,512]{0,2,1:T(8,128)(2,1)S(1)}, u32[]{:S(2)}, u32[]{:S(2)}) %all-to-all-start) | async-done | bytes 2097184 | tf_op jit(solution)/shard_map/all_to_all | solution.py:27
  425.0 0.0 copy-start
  425.0 4.5 all-to-all-start.1
  429.5 0.0 copy-done
  429.5 2.9 copy.14
  432.4 28.2 %all-to-all-done.1 = bf16[256,8,512]{0,2,1:T(8,128)(2,1)} async-done(((bf16[256,8,512]{0,2,1:T(8,128)(2,1)}), bf16[256,8,512]{0,2,1:T(8,128)(2,1)}, u32[]{:S(2)}, u32[]{:S(2)}) %all-to-all-start.1) | async-done | bytes 2097184 | tf_op jit(solution)/shard_map/all_to_all | solution.py:28
  460.6 4.1 copy.16
  464.7 5.5 %convolution_bitcast_fusion.1 = f32[512,896]{0,1:T(8,128)} fusion(bf16[2048,896]{1,0:T(8,128)(2,1)} %all-gather.13.cloned.1.call-done, bf16[2048,512]{1,0:T(8,128)(2,1)S(1)} %bitcast.30), kind=kOutput, calls=%fused_computation.2 | convolution fusion | flops 1879048192 | bytes 7602176 | tf_op jit(solution)/shard_map/dot_general | solution.py:8
  470.3 2.8 copy.17
  473.0 5.5 %convolution_bitcast_fusion = f32[512,896]{0,1:T(8,128)} fusion(bf16[2048,896]{1,0:T(8,128)(2,1)} %all-gather.15.cloned.1.call-done, bf16[2048,512]{1,0:T(8,128)(2,1)S(1)} %bitcast.31), kind=kOutput, calls=%fused_computation.1 | convolution fusion | flops 1879048192 | bytes 7602176 | tf_op jit(solution)/shard_map/dot_general | solution.py:8
  478.6 0.0 copy-start.1
  478.6 2.9 copy.18
  481.5 0.0 all-gather.17.cloned.1.call-done
  481.5 0.0 copy-done.1
  481.5 5.4 fusion.4
  486.8 47.2 %reduce-scatter.2.cloned.1.call-done = f32[128,512]{1,0:T(8,128)} async-done(((f32[2048,512]{1,0:T(8,128)}), f32[128,512]{1,0:T(8,128)}) %reduce-scatter.2.cloned.1.call-update) | async-done | bytes 262160 | tf_op jit(solution)/shard_map/reduce_scatter | solution.py:56
  534.0 1.6 convert_element_type.14
Async XLA Ops:
  7.2 87.1 %all-gather.7.cloned.1.call-start = ((), (), s32[]{:S(2)}) async-start(), calls=%async_computation.3 | async-start | bytes 8257536 | tf_op jit(solution)/shard_map/all_gather | solution.py:45
  7.9 168.9 %all-gather.11.cloned.1.call-start = ((), (), s32[]{:S(2)}) async-start(), calls=%async_computation.5 | async-start | bytes 8257536 | tf_op jit(solution)/shard_map/all_gather | solution.py:34
  8.6 250.7 %all-gather.9.cloned.1.call-start = ((), (), s32[]{:S(2)}) async-start(), calls=%async_computation.4 | async-start | bytes 8257536 | tf_op jit(solution)/shard_map/all_gather | solution.py:39
  9.4 167.4 %copy-start.2 = (bf16[256,4096]{1,0:T(8,128)(2,1)S(1)}, bf16[256,4096]{1,0:T(8,128)(2,1)}, u32[]{:S(2)}) copy-start(bf16[256,4096]{1,0:T(8,128)(2,1)} %param.5) | copy-start | bytes 6291460
  9.4 303.7 %all-gather.13.cloned.1.call-start = ((), (), s32[]{:S(2)}) async-start(), calls=%async_computation.6 | async-start | bytes 4128768 | tf_op jit(solution)/shard_map/all_gather | solution.py:52
  183.1 130.0 %copy-start.3 = (bf16[512,896]{1,0:T(8,128)(2,1)S(1)}, bf16[512,896]{1,0:T(8,128)(2,1)}, u32[]{:S(2)}) copy-start(bf16[512,896]{1,0:T(8,128)(2,1)} %param.6) | copy-start | bytes 2752516
  266.5 95.1 %all-gather.15.cloned.1.call-start = ((), (), s32[]{:S(2)}) async-start(), calls=%async_computation.7 | async-start | bytes 4128768 | tf_op jit(solution)/shard_map/all_gather | solution.py:53
  267.1 214.3 %all-gather.17.cloned.1.call-start = ((), (), s32[]{:S(2)}) async-start(), calls=%async_computation.9 | async-start | bytes 4128768 | tf_op jit(solution)/shard_map/all_gather | solution.py:51
  267.7 266.3 %reduce-scatter.2.cloned.1.call-start = ((), (), s32[]{:S(2)}) async-start(), calls=%async_computation.8 | async-start | bytes 4456448 | tf_op jit(solution)/shard_map/reduce_scatter | solution.py:56
  372.1 52.9 %all-to-all-start = ((bf16[256,8,512]{0,2,1:T(8,128)(2,1)}), bf16[256,8,512]{0,2,1:T(8,128)(2,1)S(1)}, u32[]{:S(2)}, u32[]{:S(2)}) async-start(bf16[256,8,512]{0,2,1:T(8,128)(2,1)} %bitcast.34), calls=%async_computation.1 | async-start | bytes 4194304 | tf_op jit(solution)/shard_map/all_to_all | solution.py:27
  425.0 4.5 copy-start
  425.0 35.6 %all-to-all-start.1 = ((bf16[256,8,512]{0,2,1:T(8,128)(2,1)}), bf16[256,8,512]{0,2,1:T(8,128)(2,1)}, u32[]{:S(2)}, u32[]{:S(2)}) async-start(bf16[256,8,512]{0,2,1:T(8,128)(2,1)} %bitcast.33), calls=%async_computation.2 | async-start | bytes 4194304 | tf_op jit(solution)/shard_map/all_to_all | solution.py:28
  478.6 2.9 copy-start.1
Sparse Core Ops, SparseCore 0:
  9.6 84.5 all-gather.6
  95.9 80.8 all-gather.10
  178.4 80.8 all-gather.8
  266.6 46.4 all-gather.12
  314.6 46.9 all-gather.14
  363.1 82.6 all-gather.16
  449.9 84.0 reduce-scatter.1
where the time goes:
time: 543 us; the launch traced here: 542 us
  waiting for transfers between devices  448 us (83%)
  matrix products  51.2 us (9%)
  local copies, waits for them, and re-layouts  19.3 us (4%)
  between operations  14.2 us (3%)
  starting transfers between devices  8.4 us (2%)
    all_gather x1, waiting for transfers between devices, local(): lax.all_gather(down_weight, 'grp', axis=1, tiled=True)  84.8 us
    all_gather x1, waiting for transfers between devices, local(): lax.all_gather(up_weight, 'grp', axis=0, tiled=True)  76.2 us
    all_gather x1, waiting for transfers between devices, local(): lax.all_gather(gate_weight, 'grp', axis=0, tiled=True)  75.5 us
    reduce_scatter x1, waiting for transfers between devices, local(): lax.psum_scatter(contract_cols(all_delta_gate, gate_weight) + contract_co...  47.2 us
    all_gather x1, waiting for transfers between devices, local(): lax.all_gather(delta_gate, 'grp', axis=0, tiled=True)  45.4 us
    all_to_all x1, waiting for transfers between devices, local(): lax.all_to_all(token_split, 'grp', split_axis=1, concat_axis=0, tiled=True)  45.2 us
    all_gather x1, waiting for transfers between devices, local(): lax.all_gather(delta_up, 'grp', axis=0, tiled=True)  42.1 us
    all_to_all x1, waiting for transfers between devices, local(): lax.all_to_all(grad_split, 'grp', split_axis=1, concat_axis=0, tiled=True)  28.2 us
  transfers between devices with their start and end apart: 9, of which 8 were waited for; matrix products, arithmetic and copies ran while one was open for 12% of the time, Pallas kernels for 0%

commit v1 on v0

v1 whole, which is shorter than its diff:
```python
import functools

import jax
import jax.numpy as jnp
from jax import lax
from jax.experimental import pallas as pl
from jax.experimental.pallas import tpu as pltpu
from jax.sharding import PartitionSpec as P

MESH = pl.DeviceIdType.MESH
BF16 = jnp.bfloat16
F32 = jnp.float32

Q = 224
DH = 2048
B = 512
CHUNK = 512


def dot_nt(left, right):
    return lax.dot_general(left, right, (((1,), (1,)), ((), ())), preferred_element_type=F32)


def dot_nn(left, right):
    return lax.dot_general(left, right, (((1,), (0,)), ((), ())), preferred_element_type=F32)


def dot_tn(left, right):
    return lax.dot_general(left, right, (((0,), (0,)), ((), ())), preferred_element_type=F32)


def kernel(
    tok, grd, w, dw, dx,
    buf, wbuf, part, other, acts, acc, dws, dxs, dxr, zr, ys, yr, xs, xr,
    ssem, rsem, lsem, zsem,
):
    grp, shard = lax.axis_index("grp"), lax.axis_index("shard")
    x_lo, y = lax.div(grp, 4), lax.rem(grp, 4)
    x_hi, z, c = lax.div(shard, 8), lax.rem(lax.div(shard, 2), 4), lax.rem(shard, 2)
    x = 2 * x_hi + x_lo

    def mod4(v):
        return lax.rem(v + 8, 4)

    def device(x, y, z, c):
        return (4 * lax.rem(x, 2) + y, 8 * lax.div(x, 2) + 2 * z + c)

    sibling = device(x, y, z, 1 - c)
    inner = device(x + 1 - 2 * x_lo, y, z, c)
    outer = device(mod4(x - 1 + 2 * x_lo), y, z, c)
    across = device(mod4(x + 2), y, z, c)
    along_y = {d: device(x, mod4(y + d), z, c) for d in (1, 2, 3)}
    along_z = {d: device(x, y, mod4(z + d), c) for d in (1, 2, 3)}

    barrier = pltpu.get_barrier_semaphore()
    partners = [sibling, inner, outer, across, *along_y.values(), *along_z.values()]
    for partner in partners:
        pl.semaphore_signal(barrier, inc=1, device_id=partner, device_id_type=MESH)
    pl.semaphore_wait(barrier, len(partners))

    count = [0]
    sent = []

    def push(src, dst, target, recv=None):
        n = count[0]
        count[0] += 1
        copy = pltpu.make_async_remote_copy(
            src_ref=src, dst_ref=dst, send_sem=ssem.at[n],
            recv_sem=rsem.at[n] if recv is None else recv,
            device_id=target, device_id_type=MESH,
        )
        copy.start()
        sent.append(copy)
        return copy

    local_count = [0]

    def bring(src, dst):
        n = local_count[0]
        local_count[0] += 1
        copy = pltpu.make_async_copy(src, dst, lsem.at[n])
        copy.start()
        return copy

    def rows(start, size):
        return pl.ds(pl.multiple_of(start, 32), size)

    def cols(block, size):
        return pl.ds(pl.multiple_of(block * size, size), size)

    mine, theirs = cols(x_lo, DH), cols(1 - x_lo, DH)
    own_rows, outer_rows = rows(32 * x_lo, 32), rows(32 * (1 - x_lo), 32)

    from_outer = {}
    for off in (0, 1, 3, 2):
        q = mod4(z + off)
        from_outer[off] = [
            push(src.at[c, q, :, theirs], buf.at[a, q, c, own_rows, :], outer)
            for a, src in enumerate((tok, grd))
        ]
    own = [
        bring(src.at[h, :, :, mine], buf.at[a, :, h, own_rows, :])
        for a, src in enumerate((tok, grd))
        for h in (0, 1)
    ]
    own_w = bring(w.at[:, y], wbuf.at[:, :, cols(y, B)])

    for copy in own:
        copy.wait()
    for copy in from_outer[0]:
        copy.wait_recv()
    from_y = [
        push(buf.at[:, z, c, 0:64, :], buf.at[:, z, c, 64 * (4 - d) : 64 * (5 - d), :], along_y[d])
        for d in (1, 3, 2)
    ]
    from_w = [
        push(w.at[:, mod4(y + d)], wbuf.at[:, :, cols(y, B)], along_y[d]) for d in (1, 3, 2)
    ]
    core_outer = []
    for off in (0, 1, 3, 2):
        q = mod4(z + off)
        if off:
            for copy in from_outer[off]:
                copy.wait_recv()
        part_ref = buf.at[:, q, c, outer_rows, :]
        core_outer.append(push(part_ref, part_ref, sibling))

    def piece(q):
        return buf.at[:, q, c, 64:256, :]

    for copy in from_y:
        copy.wait_recv()
    up = push(piece(z), piece(z), along_z[1])
    down = push(piece(z), piece(z), along_z[3])
    core_piece = {0: push(piece(z), piece(z), sibling)}

    own_w.wait()
    for copy in from_w:
        copy.wait_recv()

    offs = (0, 1, 3, 2)
    exchange = {}

    def forward(i):
        q = mod4(z + offs[i])

        def half(h, carry):
            at = cols(h, 256)
            weights = wbuf[...]
            part[i, 0 : 2 * Q, at] = dot_nt(
                weights[0:2].reshape(2 * Q, DH), buf[0, q, h]
            ).astype(BF16)
            part[i, 2 * Q :, at] = dot_nt(weights[2], buf[1, q, h]).astype(BF16)
            return carry

        lax.fori_loop(0, 2, half, 0)
        exchange[i] = push(part.at[i], other.at[i], inner)

    def activate(i):
        exchange[i].wait_recv()

        def some(r, carry):
            def full(m):
                at = pl.ds(pl.multiple_of(m * Q + 32 * r, 32), 32)
                return part[i, at, :].astype(F32) + other[i, at, :].astype(F32)

            gate, up_pre, back = full(0), full(1), full(2)
            s = jax.nn.sigmoid(gate)
            silu = gate * s

            def put(m, value):
                acts[i, pl.ds(pl.multiple_of(m * Q + 32 * r, 32), 32), :] = value.astype(BF16)

            put(0, back * up_pre * s * (1.0 + gate * (1.0 - s)))
            put(1, back * silu)
            put(2, silu * up_pre)
            return carry

        lax.fori_loop(0, Q // 32, some, 0)

    def weight_terms(i, n):
        q = mod4(z + offs[i])
        at = cols(n, B)
        return (
            dot_nn(acts[i, 0 : 2 * Q, :], buf[0, q, :, :, at].reshape(CHUNK, B)),
            dot_nn(acts[i, 2 * Q :, :], buf[1, q, :, :, at].reshape(CHUNK, B)),
        )

    def weight_grads(i):
        def block(n, carry):
            both, third = weight_terms(i, n)
            at = cols(n, B)
            if i:
                both = both + acc[0 : 2 * Q, at]
                third = third + acc[2 * Q :, at]
            acc[0 : 2 * Q, at] = both
            acc[2 * Q :, at] = third
            return carry

        lax.fori_loop(0, 4, block, 0)

    from_dw = []

    def last_weight_grads(i):
        for d in (1, 3, 2, 0):
            n = mod4(y + d)
            both, third = weight_terms(i, n)
            at = cols(n, B)
            dws[n, 0:2] = (both + acc[0 : 2 * Q, at]).astype(BF16).reshape(2, Q, B)
            dws[n, 2] = (third + acc[2 * Q :, at]).astype(BF16)
            if d:
                from_dw.append(push(dws.at[n], dw.at[:, y], along_y[d]))
        return bring(dws.at[y], dw.at[:, y])

    core_dx = {}

    def token_grads(i):
        def block(n, carry):
            at = cols(n, B)
            weights = wbuf[0:2, :, at].reshape(2 * Q, B)
            for h in (0, 1):
                left = acts[i, 0 : 2 * Q, 256 * h : 256 * h + 256]
                dxs[i, h, :, at] = dot_tn(left, weights).astype(BF16)
            return carry

        lax.fori_loop(0, 4, block, 0)
        core_dx[i] = push(dxs.at[i, 1 - c], dxr.at[i], sibling)

    from_z = []

    def along_z_grads(i):
        q = mod4(z + offs[i])
        core_dx[i].wait_recv()

        def some(r, carry):
            at = rows(32 * r, 32)
            dxs[i, c, at, :] = (
                dxs[i, c, at, :].astype(F32) + dxr[i, at, :].astype(F32)
            ).astype(BF16)
            return carry

        lax.fori_loop(0, 8, some, 0)
        for d in (1, 3, 2):
            at = rows(64 * mod4(z + d - y), 64)
            push(dxs.at[i, c, at, :], zr.at[q, d - 1], along_z[d], zsem.at[q, d - 1])

    for copy in core_outer:
        copy.wait_recv()
    core_piece[0].wait_recv()
    forward(0)
    up.wait_recv()
    q = mod4(z + 3)
    on_up = push(buf.at[0, q, c, 64:256, :], buf.at[0, q, c, 64:256, :], along_z[1])
    core_piece[3] = push(piece(q), piece(q), sibling)
    down.wait_recv()
    q = mod4(z + 1)
    on_down = push(buf.at[1, q, c, 64:256, :], buf.at[1, q, c, 64:256, :], along_z[3])
    core_piece[1] = push(piece(q), piece(q), sibling)
    core_piece[3].wait_recv()
    core_piece[1].wait_recv()
    forward(1)
    forward(2)
    activate(0)
    weight_grads(0)
    token_grads(0)
    on_up.wait_recv()
    on_down.wait_recv()
    q = mod4(z + 2)
    core_piece[2] = push(piece(q), piece(q), sibling)
    along_z_grads(0)
    core_piece[2].wait_recv()
    forward(3)
    activate(1)
    weight_grads(1)
    token_grads(1)
    activate(2)
    along_z_grads(1)
    weight_grads(2)
    token_grads(2)
    activate(3)
    along_z_grads(2)
    own_dw = last_weight_grads(3)
    token_grads(3)
    along_z_grads(3)

    from_yg = {}
    for i in range(4):
        q = mod4(z + offs[i])
        for d in (1, 2, 3):
            pltpu.make_async_remote_copy(
                src_ref=zr.at[q, d - 1], dst_ref=zr.at[q, d - 1], send_sem=ssem.at[0],
                recv_sem=zsem.at[q, d - 1], device_id=along_z[d], device_id_type=MESH,
            ).wait_recv()
    for i in range(4):
        q = mod4(z + offs[i])
        keep = rows(64 * mod4(z - y), 64)
        total = dxs[i, c, keep, :].astype(F32)
        for d in (0, 1, 2):
            total = total + zr[q, d].astype(F32)
        ys[i] = total.astype(BF16)
        for d in (1, 3, 2):
            from_yg[i, d] = push(ys.at[i, :, cols(mod4(y + d), B)], yr.at[i, d - 1], along_y[d])
    for i in range(4):
        q = mod4(z + offs[i])
        total = ys[i, :, cols(y, B)].astype(F32)
        for d in (1, 2, 3):
            from_yg[i, d].wait_recv()
            total = total + yr[i, d - 1].astype(F32)
        xs[0, q] = total[0:32].astype(BF16)
        xs[1, q] = total[32:64].astype(BF16)
    from_x = push(xs.at[1 - x_hi], xr, across)
    from_x.wait_recv()
    dx[...] = (xs[x_hi].astype(F32) + xr[...].astype(F32)).astype(BF16).reshape(128, B)

    own_dw.wait()
    for copy in from_dw:
        copy.wait_recv()
    for copy in sent:
        copy.wait_send()


def local(tokens, gate_weight, up_weight, down_weight, grad_out):
    w = jnp.stack([gate_weight.T, up_weight.T, down_weight]).reshape(3, 4, Q, B)
    flops = 8 * 2 * 2048 * 2048 * 256
    dw, dx = pl.pallas_call(
        kernel,
        out_shape=(
            jax.ShapeDtypeStruct((3, 4, Q, B), BF16),
            jax.ShapeDtypeStruct((128, B), BF16),
        ),
        in_specs=[pl.BlockSpec(memory_space=pl.ANY)] * 3,
        out_specs=(
            pl.BlockSpec(memory_space=pl.ANY),
            pl.BlockSpec(memory_space=pltpu.VMEM),
        ),
        scratch_shapes=[
            pltpu.VMEM((2, 4, 2, 256, DH), BF16),
            pltpu.VMEM((3, Q, DH), BF16),
            pltpu.VMEM((4, 3 * Q, CHUNK), BF16),
            pltpu.VMEM((4, 3 * Q, CHUNK), BF16),
            pltpu.VMEM((4, 3 * Q, CHUNK), BF16),
            pltpu.VMEM((3 * Q, DH), F32),
            pltpu.VMEM((4, 3, Q, B), BF16),
            pltpu.VMEM((4, 2, 256, DH), BF16),
            pltpu.VMEM((4, 256, DH), BF16),
            pltpu.VMEM((4, 3, 64, DH), BF16),
            pltpu.VMEM((4, 64, DH), BF16),
            pltpu.VMEM((4, 3, 64, B), BF16),
            pltpu.VMEM((2, 4, 32, B), BF16),
            pltpu.VMEM((4, 32, B), BF16),
            pltpu.SemaphoreType.DMA((72,)),
            pltpu.SemaphoreType.DMA((72,)),
            pltpu.SemaphoreType.DMA((8,)),
            pltpu.SemaphoreType.DMA((4, 3)),
        ],
        compiler_params=pltpu.CompilerParams(
            collective_id=0, has_side_effects=True, vmem_limit_bytes=60 * 2**20
        ),
        cost_estimate=pl.CostEstimate(flops=flops, bytes_accessed=2**24, transcendentals=2**20),
    )(tokens.reshape(2, 4, 32, 4096), grad_out.reshape(2, 4, 32, 4096), w)
    dw = dw.reshape(3, 4 * Q, B)
    return (dx, dw[0].T.astype(F32), dw[1].T.astype(F32), dw[2].astype(F32))


def solution(mesh):
    return jax.shard_map(
        local,
        mesh=mesh,
        in_specs=(
            P("grp", None),
            P("grp", "shard"),
            P("grp", "shard"),
            P("shard", "grp"),
            P("grp", None),
        ),
        out_specs=(P("shard", "grp"), P("grp", "shard"), P("grp", "shard"), P("shard", "grp")),
        check_vma=False,
    )
```

time: 543 us -> 195 us (0.36)
  waiting for transfers between devices: 448 us -> 0 us
  Pallas kernels: 0 us -> 178 us
  matrix products: 51.2 us -> 0 us
  between operations: 14.2 us -> 0.68 us
  local copies, waits for them, and re-layouts: 19.3 us -> 8.98 us
  starting transfers between devices: 8.4 us -> 0 us
    all_gather x6 -> x0, waiting for transfers between devices: 324 us -> none  [the longest x1 84.8 us: local(): lax.all_gather(down_weight, 'grp', axis=1, tiled=True)]
    pallas_call x0 -> x1, Pallas kernels: none -> 178 us  [local(): pl.pallas_call(kernel, out_shape=(jax.ShapeDtypeStruct((3, 4, Q, B), BF16...]
    all_to_all x2 -> x0, waiting for transfers between devices: 73.4 us -> none  [the longest x1 45.2 us: local(): lax.all_to_all(token_split, 'grp', split_axis=1, concat_axis=0, tiled=True)]
    dot_general x8 -> x0, matrix products: 51.2 us -> none  [the longest x3 21.3 us: contract_cols(): lax.dot_general(left, right, (((1,), (1,)), ((), ())), preferred_element_...]
    reduce_scatter x1 -> x0, waiting for transfers between devices: 47.2 us -> none  [local(): lax.psum_scatter(contract_cols(all_delta_gate, gate_weight) + contract_co...]
    unnamed x12 -> x5, local copies, waits for them, and re-layouts: 12.3 us -> 0.66 us
    all_to_all x2 -> x0, starting transfers between devices: 8.13 us -> none  [the longest x1 4.53 us: local(): lax.all_to_all(grad_split, 'grp', split_axis=1, concat_axis=0, tiled=True)]
    all_to_all x2 -> x0, local copies, waits for them, and re-layouts: 7 us -> none  [the longest x1 4.12 us: local(): lax.all_to_all(grad_split, 'grp', split_axis=1, concat_axis=0, tiled=True)]
  transfers between devices with their start and end apart: 9 -> 0, of which waited for: 8 -> 0; matrix products, arithmetic and copies ran while one was open for 12% -> 0% of each run, Pallas kernels for 0% -> 0%
where the time goes in v1:
time: 195 us; the launch traced here: 194 us
  Pallas kernels  178 us (91%)
  local copies, waits for them, and re-layouts  8.98 us (5%)
  other arithmetic  6.31 us (3%)
    pallas_call x1, Pallas kernels, local(): pl.pallas_call(kernel, out_shape=(jax.ShapeDtypeStruct((3, 4, Q, B), BF16...  178 us

profile of v1, /device:TPU:0, one launch (start us, length us, event | category | flops | bytes accessed | tf_op | source)
XLA Modules:
  0.0 193.9 jit_solution(9569570774865599529)
XLA Ops:
  0.6 0.0 copy-start
  0.6 1.5 copy.9
  2.2 0.0 copy-done
  2.2 0.5 copy.10
  2.7 3.0 %pad_maximum_fusion.w = bf16[3,4,224,512]{3,2,1,0:T(8,128)(2,1)} fusion(bf16[1,4,224,512]{3,2,1,0:T(8,128)(2,1)} %bitcast.24, bf16[1,4,224,512]{3,2,1,0:T(8,128)(2,1)S(1)} %bitcast.19, bf16[1,4,224,512]{3,2,1,0:T(8,128)(2,1)S(1)} %bitcast.18), kind=kLoop, calls=%fused_computation | loop fusion | flops 2752512 | bytes 5505024 | tf_op jit(solution)/shard_map/stack | solution.py:323
  5.8 178.0 %shard_map.84 = (bf16[3,4,224,512]{3,2,1,0:T(8,128)(2,1)}, bf16[128,512]{1,0:T(8,128)(2,1)}) custom-call(bf16[2,4,32,4096]{3,2,1,0:T(8,128)(2,1)} %bitcast.25, bf16[2,4,32,4096]{3,2,1,0:T(8,128)(2,1)} %bitcast.26, bf16[3,4,224,512]{3,2,1,0:T(8,128)(2,1)} %pad_maximum_fusion.w), custom_call_target="tpu_custom_call" | custom-call | flops 17179869184 | bytes 16777216 | tf_op jit(solution)/shard_map/pallas_call | solution.py:325
  183.7 2.9 %fusion = (bf16[1,4,224,512]{3,2,1,0:T(8,128)(2,1)S(1)}, bf16[1,4,224,512]{3,2,1,0:T(8,128)(2,1)}, bf16[1,4,224,512]{3,2,1,0:T(8,128)(2,1)S(1)}) fusion(bf16[3,4,224,512]{3,2,1,0:T(8,128)(2,1)} %get-tuple-element.7), kind=kLoop, calls=%fused_computation.4 | loop fusion | bytes 5505024 | tf_op jit(solution)/shard_map/slice | solution.py:362
  186.6 0.3 bitcast_convert_fusion.2
  186.9 1.7 copy.11
  188.6 3.0 %bitcast_convert_fusion = (f32[896,512]{1,0:T(8,128)}, f32[896,512]{1,0:T(8,128)S(1)}) fusion(bf16[1,4,224,512]{3,2,1,0:T(8,128)(2,1)S(1)} %get-tuple-element.8, bf16[1,4,224,512]{3,2,1,0:T(8,128)(2,1)} %get-tuple-element.9), kind=kLoop, calls=%fused_computation.1 | loop fusion | flops 917504 | bytes 5505024 | tf_op jit(solution)/shard_map/convert_element_type | solution.py:362
  191.6 0.0 copy-start.1
  191.6 1.7 copy.12
  193.3 0.0 copy-done.1
  193.3 0.7 copy.14
Async XLA Ops:
  0.6 1.6 copy-start
  191.6 1.7 copy-start.1

commit v2 on v1

v2 whole, which is shorter than its diff:
```python
import functools

import jax
import jax.numpy as jnp
from jax import lax
from jax.experimental import pallas as pl
from jax.experimental.pallas import tpu as pltpu
from jax.sharding import PartitionSpec as P

MESH = pl.DeviceIdType.MESH
BF16 = jnp.bfloat16
F32 = jnp.float32

Q = 224
DH = 2048
B = 512
CHUNK = 512
PARTS = ((0, 112), (112, 112))
PARTS = ((0, 112), (112, 112))
PARTS = ((0, 112), (112, 112))


def dot_nt(left, right):
    return lax.dot_general(left, right, (((1,), (1,)), ((), ())), preferred_element_type=F32)


def dot_nn(left, right):
    return lax.dot_general(left, right, (((1,), (0,)), ((), ())), preferred_element_type=F32)


def dot_tn(left, right):
    return lax.dot_general(left, right, (((0,), (0,)), ((), ())), preferred_element_type=F32)


def kernel(
    tok, grd, gate_w, up_w, down_w, dgate, dup, ddown, dx,
    buf, raw, wt, wbuf, part, other, acc, back, dxs, dxr, zr, ys, yr, xs, xr,
    ssem, rsem, lsem, zsem, lastsem,
):
    grp, shard = lax.axis_index("grp"), lax.axis_index("shard")
    x_lo, y = lax.div(grp, 4), lax.rem(grp, 4)
    x_hi, z, c = lax.div(shard, 8), lax.rem(lax.div(shard, 2), 4), lax.rem(shard, 2)
    x = 2 * x_hi + x_lo

    def mod4(v):
        return lax.rem(v + 8, 4)

    def slot(dy):
        return dy + lax.div(dy, 2) * (1 - 2 * lax.rem(dy, 2))

    def device(x, y, z, c):
        return (4 * lax.rem(x, 2) + y, 8 * lax.div(x, 2) + 2 * z + c)

    sibling = device(x, y, z, 1 - c)
    inner = device(x + 1 - 2 * x_lo, y, z, c)
    outer = device(mod4(x - 1 + 2 * x_lo), y, z, c)
    across = device(mod4(x + 2), y, z, c)
    along_y = {d: device(x, mod4(y + d), z, c) for d in (1, 2, 3)}
    along_z = {d: device(x, y, mod4(z + d), c) for d in (1, 2, 3)}

    barrier = pltpu.get_barrier_semaphore()
    partners = [sibling, inner, outer, across, *along_y.values(), *along_z.values()]
    for partner in partners:
        pl.semaphore_signal(barrier, inc=1, device_id=partner, device_id_type=MESH)
    pl.semaphore_wait(barrier, len(partners))

    count = [0]
    sent = []

    def push(src, dst, target, recv=None):
        n = count[0]
        count[0] += 1
        copy = pltpu.make_async_remote_copy(
            src_ref=src, dst_ref=dst, send_sem=ssem.at[n],
            recv_sem=rsem.at[n] if recv is None else recv,
            device_id=target, device_id_type=MESH,
        )
        copy.start()
        sent.append(copy)
        return copy

    local_count = [0]

    def bring(src, dst):
        n = local_count[0]
        local_count[0] += 1
        copy = pltpu.make_async_copy(src, dst, lsem.at[n])
        copy.start()
        return copy

    def arrived(*copies):
        for copy in copies:
            copy.wait_recv()

    gone = set()

    def left(*copies):
        for copy in copies:
            if id(copy) not in gone:
                gone.add(id(copy))
                copy.wait_send()

    def rows(start, size, step=32):
        return pl.ds(pl.multiple_of(start, step), size)

    def cols(block, size):
        return pl.ds(pl.multiple_of(block * size, size), size)

    mine, theirs = cols(x_lo, DH), cols(1 - x_lo, DH)
    own_rows, outer_rows = rows(32 * x_lo, 32), rows(32 * (1 - x_lo), 32)
    offs = (0, 1, 3, 2)
    quarter = [mod4(z + off) for off in offs]

    from_outer = [
        [
            push(src.at[c, q, :, theirs], buf.at[a, q, c, own_rows, :], outer)
            for a, src in enumerate((tok, grd))
        ]
        for q in quarter
    ]
    own_tok = [
        bring(src.at[h, :, :, mine], buf.at[a, :, h, own_rows, :])
        for h in (0, 1)
        for a, src in enumerate((tok, grd))
    ]
    own_raw = [bring(gate_w, raw.at[0]), bring(up_w, raw.at[1]), bring(down_w, wt.at[2])]

    for copy in own_tok:
        copy.wait()
    arrived(*from_outer[0])

    def send_y(d):
        at = {1: 2, 3: 1, 2: 3}[d] * 64
        return push(buf.at[:, z, c, 0:64, :], buf.at[:, z, c, at : at + 64, :], along_y[d])

    y_near = [send_y(1), send_y(3)]
    y_far = send_y(2)

    def outer_to_sibling(i):
        ref = buf.at[:, quarter[i], c, outer_rows, :]
        return push(ref, ref, sibling)

    core_outer = [outer_to_sibling(0)]

    for copy in own_raw:
        copy.wait()
    for m in (0, 1):
        def turn(n, carry):
            wt[m, cols(n, 128), :] = raw[m, :, cols(n, 128)].T
            return carry

        lax.fori_loop(0, 7, turn, 0)
    own_w = bring(wt.at[:, rows(Q * y, Q), :], wbuf.at[:, :, cols(y, B)])

    def near(a, q):
        return buf.at[a, q, c, 64:192, :]

    def far(a, q):
        return buf.at[a, q, c, 192:256, :]

    both = slice(None)
    core_piece = {}

    def to_sibling(i, which, a=both):
        ref = which(a, quarter[i])
        core_piece.setdefault(i, []).append(push(ref, ref, sibling))

    def spread(which):
        ref = which(both, z)
        return push(ref, ref, along_z[1]), push(ref, ref, along_z[3])

    arrived(*y_near)
    near_up, near_down = spread(near)
    to_sibling(0, near)
    for i in (1, 2, 3):
        arrived(*from_outer[i])
        core_outer.append(outer_to_sibling(i))
    arrived(y_far)
    far_up, far_down = spread(far)
    to_sibling(0, far)

    def send_w(h):
        start, size = PARTS[h]
        return [
            push(
                wt.at[:, rows(Q * mod4(y + d) + start, size, 16), :],
                wbuf.at[:, start : start + size, cols(y, B)],
                along_y[d],
            )
            for d in (1, 3, 2)
        ]

    from_w = [send_w(h) for h in range(len(PARTS))]

    def onward(which, up, down):
        arrived(up)
        ref = which(0, quarter[2])
        on_up = push(ref, ref, along_z[1])
        to_sibling(2, which)
        arrived(down)
        ref = which(1, quarter[1])
        on_down = push(ref, ref, along_z[3])
        to_sibling(1, which)
        return on_up, on_down

    exchange = {}

    def forward(i, h):
        q = quarter[i]
        start, size = PARTS[h]
        hidden = slice(start, start + size)

        def half(g, carry):
            at = cols(g, 256)
            part[i, 0:2, hidden, at] = dot_nt(
                wbuf[0:2, hidden, :].reshape(2 * size, DH), buf[0, q, g]
            ).astype(BF16).reshape(2, size, 256)
            part[i, 2, hidden, at] = dot_nt(wbuf[2, hidden, :], buf[1, q, g]).astype(BF16)
            return carry

        lax.fori_loop(0, 2, half, 0)
        exchange[i, h] = push(part.at[i, :, hidden, :], other.at[i, :, hidden, :], inner)

    def activate(i, h):
        arrived(exchange[i, h])
        left(exchange[i, h])
        start, size = PARTS[h]

        def some(r, carry):
            at = rows(start + 16 * r, 16, 16)

            def full(m):
                return part[i, m, at, :].astype(F32) + other[i, m, at, :].astype(F32)

            gate, up_pre, back_grad = full(0), full(1), full(2)
            s = jax.nn.sigmoid(gate)
            silu = gate * s
            part[i, 0, at, :] = (back_grad * up_pre * s * (1.0 + gate * (1.0 - s))).astype(BF16)
            part[i, 1, at, :] = (back_grad * silu).astype(BF16)
            part[i, 2, at, :] = (silu * up_pre).astype(BF16)
            return carry

        lax.fori_loop(0, size // 16, some, 0)

    def weight_terms(i, h, n):
        q = quarter[i]
        start, size = PARTS[h]
        hidden = slice(start, start + size)
        at = cols(n, B)
        return (
            dot_nn(
                part[i, 0:2, hidden, :].reshape(2 * size, CHUNK),
                buf[0, q, :, :, at].reshape(CHUNK, B),
            ).reshape(2, size, B),
            dot_nn(part[i, 2, hidden, :], buf[1, q, :, :, at].reshape(CHUNK, B)),
        )

    def weight_grads(i, h):
        start, size = PARTS[h]
        hidden = slice(start, start + size)

        def block(n, carry):
            pair, third = weight_terms(i, h, n)
            at = cols(n, B)
            if i:
                pair = pair + acc[0:2, hidden, at]
                third = third + acc[2, hidden, at]
            acc[0:2, hidden, at] = pair
            acc[2, hidden, at] = third
            return carry

        lax.fori_loop(0, 4, block, 0)

    from_dw, own_dw = {}, []

    def last_weight_grads(i, h):
        if h == 0:
            for copies in from_w:
                for copy in copies:
                    left(copy)
        start, size = PARTS[h]
        hidden = slice(start, start + size)
        from_dw[h] = []
        for d in (1, 3, 2, 0):
            n = mod4(y + d)
            pair, third = weight_terms(i, h, n)
            at = cols(n, B)
            held = rows(Q * n + start, size, 16)
            wt[0:2, held, :] = (pair + acc[0:2, hidden, at]).astype(BF16)
            wt[2, held, :] = (third + acc[2, hidden, at]).astype(BF16)
            there = rows(Q * y + start, size, 16)
            if d:
                from_dw[h].append(push(wt.at[0:2, held, :], back.at[:, there, :], along_y[d]))
                from_dw[h].append(push(wt.at[2, held, :], ddown.at[there, :], along_y[d]))
            else:
                own_dw.append(bring(wt.at[0:2, held, :], back.at[:, there, :]))
                own_dw.append(bring(wt.at[2, held, :], ddown.at[there, :]))

    def token_terms(i, n, g):
        at = cols(n, B)
        return dot_tn(
            part[i, 0:2, :, 256 * g : 256 * g + 256].reshape(2 * Q, 256),
            wbuf[0:2, :, at].reshape(2 * Q, B),
        ).astype(BF16)

    core_dx = {}

    def token_grads(i):
        def block(n, carry):
            for g in (0, 1):
                dxs[i, g, :, cols(n, B)] = token_terms(i, n, g)
            return carry

        lax.fori_loop(0, 4, block, 0)
        core_dx[i] = push(dxs.at[i, 1 - c], dxr.at[i], sibling)

    def z_rows(d):
        return rows(64 * slot(mod4(z + d - y)), 64)

    def along_z_grads(i):
        arrived(core_dx[i])

        def some(r, carry):
            at = rows(32 * r, 32)
            dxs[i, c, at, :] = (
                dxs[i, c, at, :].astype(F32) + dxr[i, at, :].astype(F32)
            ).astype(BF16)
            return carry

        lax.fori_loop(0, 8, some, 0)
        for d in (1, 3, 2):
            push(
                dxs.at[i, c, z_rows(d), :], zr.at[quarter[i], d - 1], along_z[d],
                zsem.at[quarter[i], d - 1],
            )

    def last_token_grads(i):
        core_last = {}
        for d in (1, 3, 2, 0):
            n = mod4(y + d)
            for g in (0, 1):
                dxs[i, g, :, cols(n, B)] = token_terms(i, n, g)
            core_last[d] = push(
                dxs.at[i, 1 - c, :, cols(n, B)], dxr.at[i, :, cols(n, B)], sibling
            )
        return core_last

    def last_along_z(i, core_last):
        for k, d in enumerate((1, 3, 2, 0)):
            at = cols(mod4(y + d), B)
            arrived(core_last[d])
            dxs[i, c, :, at] = (
                dxs[i, c, :, at].astype(F32) + dxr[i, :, at].astype(F32)
            ).astype(BF16)
            for e in (1, 3, 2):
                push(
                    dxs.at[i, c, z_rows(e), at], zr.at[quarter[i], e - 1, :, at], along_z[e],
                    lastsem.at[k, e - 1],
                )

    near_on = onward(near, near_up, near_down)
    arrived(*core_outer, *core_piece[0])
    own_w.wait()
    arrived(*from_w[0])
    forward(0, 0)
    far_on = onward(far, far_up, far_down)
    arrived(*core_piece[1])
    forward(1, 0)
    arrived(*core_piece[2])
    forward(2, 0)
    arrived(*from_w[1])
    forward(0, 1)
    activate(0, 0)
    weight_grads(0, 0)
    arrived(*near_on)
    to_sibling(3, near)
    activate(1, 0)
    weight_grads(1, 0)
    arrived(*far_on)
    to_sibling(3, far)
    arrived(*core_piece[3])
    forward(3, 0)
    forward(1, 1)
    forward(2, 1)
    forward(3, 1)
    activate(2, 0)
    weight_grads(2, 0)
    activate(0, 1)
    token_grads(0)
    weight_grads(0, 1)
    activate(3, 0)
    last_weight_grads(3, 0)
    along_z_grads(0)
    activate(1, 1)
    token_grads(1)
    weight_grads(1, 1)
    along_z_grads(1)
    activate(2, 1)
    token_grads(2)
    weight_grads(2, 1)
    along_z_grads(2)
    activate(3, 1)
    core_last = last_token_grads(3)
    last_weight_grads(3, 1)
    last_along_z(3, core_last)

    def landed(ref, sem):
        pltpu.make_async_remote_copy(
            src_ref=ref, dst_ref=ref, send_sem=ssem.at[0], recv_sem=sem,
            device_id=along_z[1], device_id_type=MESH,
        ).wait_recv()

    for d in (1, 2, 3):
        for off in (0, 1, 3):
            q = mod4(z - d + off)
            landed(zr.at[q, d - 1], zsem.at[q, d - 1])
    keep = z_rows(0)
    from_yg = {}
    for k, d in enumerate((1, 3, 2, 0)):
        at = cols(mod4(y + d), B)
        for e in (1, 2, 3):
            landed(zr.at[mod4(z - e + 2), e - 1, :, at], lastsem.at[k, e - 1])

        for i in range(4):
            q = quarter[i]
            total = dxs[i, c, keep, at].astype(F32)
            for e in (0, 1, 2):
                total = total + zr[q, e, :, at].astype(F32)
            ys[q, :, at] = total.astype(BF16)
        if d:
            from_yg[d] = push(ys.at[:, :, at], yr.at[d - 1], along_y[d])
    for copy in own_dw:
        copy.wait()
    arrived(*from_dw[0], *from_dw[1])
    for m, out in enumerate((dgate, dup)):
        def turn(n, carry):
            out[:, cols(n, 128)] = back[m, cols(n, 128), :].T
            return carry

        lax.fori_loop(0, 7, turn, 0)
    for d in (1, 3, 2):
        arrived(from_yg[d])
    for q in range(4):
        total = ys[q, :, cols(y, B)].astype(F32)
        for d in (0, 1, 2):
            total = total + yr[d, q].astype(F32)
        xs[0, q] = total[0:32].astype(BF16)
        xs[1, q] = total[32:64].astype(BF16)
    from_x = push(xs.at[1 - x_hi], xr, across)
    arrived(from_x)
    dx[...] = (xs[x_hi].astype(F32) + xr[...].astype(F32)).astype(BF16).reshape(128, B)
    left(*sent)


def local(tokens, gate_weight, up_weight, down_weight, grad_out):
    flops = 8 * 2 * 2048 * 2048 * 256
    dgate, dup, ddown, dx = pl.pallas_call(
        kernel,
        out_shape=(
            jax.ShapeDtypeStruct((B, 4 * Q), BF16),
            jax.ShapeDtypeStruct((B, 4 * Q), BF16),
            jax.ShapeDtypeStruct((4 * Q, B), BF16),
            jax.ShapeDtypeStruct((128, B), BF16),
        ),
        in_specs=[pl.BlockSpec(memory_space=pl.ANY)] * 5,
        out_specs=(
            pl.BlockSpec(memory_space=pltpu.VMEM),
            pl.BlockSpec(memory_space=pltpu.VMEM),
            pl.BlockSpec(memory_space=pl.ANY),
            pl.BlockSpec(memory_space=pltpu.VMEM),
        ),
        scratch_shapes=[
            pltpu.VMEM((2, 4, 2, 256, DH), BF16),
            pltpu.VMEM((2, B, 4 * Q), BF16),
            pltpu.VMEM((3, 4 * Q, B), BF16),
            pltpu.VMEM((3, Q, DH), BF16),
            pltpu.VMEM((4, 3, Q, CHUNK), BF16),
            pltpu.VMEM((4, 3, Q, CHUNK), BF16),
            pltpu.VMEM((3, Q, DH), F32),
            pltpu.VMEM((2, 4 * Q, B), BF16),
            pltpu.VMEM((4, 2, 256, DH), BF16),
            pltpu.VMEM((4, 256, DH), BF16),
            pltpu.VMEM((4, 3, 64, DH), BF16),
            pltpu.VMEM((4, 64, DH), BF16),
            pltpu.VMEM((3, 4, 64, B), BF16),
            pltpu.VMEM((2, 4, 32, B), BF16),
            pltpu.VMEM((4, 32, B), BF16),
            pltpu.SemaphoreType.DMA((96,)),
            pltpu.SemaphoreType.DMA((96,)),
            pltpu.SemaphoreType.DMA((16,)),
            pltpu.SemaphoreType.DMA((4, 3)),
            pltpu.SemaphoreType.DMA((4, 3)),
        ],
        compiler_params=pltpu.CompilerParams(
            collective_id=0, has_side_effects=True, vmem_limit_bytes=62 * 2**20
        ),
        cost_estimate=pl.CostEstimate(flops=flops, bytes_accessed=2**24, transcendentals=2**20),
    )(
        tokens.reshape(2, 4, 32, 4096), grad_out.reshape(2, 4, 32, 4096),
        gate_weight, up_weight, down_weight,
    )
    return (dx, dgate.astype(F32), dup.astype(F32), ddown.astype(F32))


def solution(mesh):
    return jax.shard_map(
        local,
        mesh=mesh,
        in_specs=(
            P("grp", None),
            P("grp", "shard"),
            P("grp", "shard"),
            P("shard", "grp"),
            P("grp", None),
        ),
        out_specs=(P("shard", "grp"), P("grp", "shard"), P("grp", "shard"), P("shard", "grp")),
        check_vma=False,
    )
```

time: 195 us -> 172 us (0.88)
  Pallas kernels: 178 us -> 164 us
  local copies, waits for them, and re-layouts: 8.98 us -> 0.82 us
    pallas_call x1, Pallas kernels: 178 us -> 164 us  [local(): pl.pallas_call(kernel, out_shape=(jax.ShapeDtypeStruct((B, 4 * Q), BF16),...]
    convert_element_type x2 -> x0, local copies, waits for them, and re-layouts: 3.36 us -> none  [local(): return (dx, dw[0].T.astype(F32), dw[1].T.astype(F32), dw[2].astype(F32))]
    another operation x1 -> x0, other arithmetic: 3.03 us -> none  [local(): w = jnp.stack([gate_weight.T, up_weight.T, down_weight]).reshape(3, 4, Q, B)]
    slice x1 -> x0, local copies, waits for them, and re-layouts: 2.89 us -> none  [local(): return (dx, dw[0].T.astype(F32), dw[1].T.astype(F32), dw[2].astype(F32))]
    convert_element_type x2 -> x3, other arithmetic: 3.28 us -> 5.45 us  [local(): return (dx, dgate.astype(F32), dup.astype(F32), ddown.astype(F32))]
    transpose x2 -> x0, local copies, waits for them, and re-layouts: 2.07 us -> none  [local(): w = jnp.stack([gate_weight.T, up_weight.T, down_weight]).reshape(3, 4, Q, B)]
where the time goes in v2:
time: 172 us; the launch traced here: 171 us
  Pallas kernels  164 us (95%)
  other arithmetic  5.45 us (3%)
    pallas_call x1, Pallas kernels, local(): pl.pallas_call(kernel, out_shape=(jax.ShapeDtypeStruct((B, 4 * Q), BF16),...  164 us
    convert_element_type x3, other arithmetic, local(): return (dx, dgate.astype(F32), dup.astype(F32), ddown.astype(F32))  5.45 us

profile of v2, /device:TPU:0, one launch (start us, length us, event | category | flops | bytes accessed | tf_op | source)
XLA Modules:
  0.0 170.5 jit_solution(17631588237446248932)
XLA Ops:
  0.6 163.6 %shard_map.84 = (bf16[512,896]{1,0:T(8,128)(2,1)}, bf16[512,896]{1,0:T(8,128)(2,1)}, bf16[896,512]{1,0:T(8,128)(2,1)}, bf16[128,512]{1,0:T(8,128)(2,1)}) custom-call(bf16[2,4,32,4096]{3,2,1,0:T(8,128)(2,1)} %bitcast.2, bf16[2,4,32,4096]{3,2,1,0:T(8,128)(2,1)} %bitcast.3, bf16[512,896]{1,0:T(8,128)(2,1)} %gate_w.1, bf16[512,896]{1,0:T(8,128)(2,1)} %up_w.1, ...), custom_call_target="tpu_custom_call" | custom-call | flops 17179869184 | bytes 16777216 | tf_op jit(solution)/shard_map/pallas_call | solution.py:457
  164.2 0.0 copy-start.1
  164.2 2.6 %convert_element_type.9 = f32[512,896]{1,0:T(8,128)} convert(bf16[512,896]{1,0:T(8,128)(2,1)} %get-tuple-element.9) | non-fusion elementwise | flops 458752 | bytes 2752512 | tf_op jit(solution)/shard_map/convert_element_type | solution.py:502
  166.8 0.0 copy-done.1
  166.8 0.0 copy-start
  166.8 1.4 convert_element_type.10
  168.2 0.2 copy-done
  168.4 0.0 copy-start.2
  168.4 1.5 convert_element_type.11
  169.8 0.0 copy-done.2
  169.8 0.7 copy.10
Async XLA Ops:
  164.2 2.6 %copy-start.1 = (bf16[512,896]{1,0:T(8,128)(2,1)S(1)}, bf16[512,896]{1,0:T(8,128)(2,1)}, u32[]{:S(2)}) copy-start(bf16[512,896]{1,0:T(8,128)(2,1)} %get-tuple-element.10) | copy-start | bytes 2752516
  166.8 1.5 copy-start
  168.4 1.5 copy-start.2

commit v3 on v2

--- a/solution.py
+++ b/solution.py
@@ -15,9 +15,7 @@
 DH = 2048
 B = 512
 CHUNK = 512
-PARTS = ((0, 112), (112, 112))
-PARTS = ((0, 112), (112, 112))
-PARTS = ((0, 112), (112, 112))
+PARTS = ((0, 128), (128, 96))
 
 
 def dot_nt(left, right):
@@ -34,7 +32,7 @@
 
 def kernel(
     tok, grd, gate_w, up_w, down_w, dgate, dup, ddown, dx,
-    buf, raw, wt, wbuf, part, other, acc, back, dxs, dxr, zr, ys, yr, xs, xr,
+    buf, raw, wt, wbuf, part, other, acc, back, dxs, dxr, zr, ys, xr, yr,
     ssem, rsem, lsem, zsem, lastsem,
 ):
     grp, shard = lax.axis_index("grp"), lax.axis_index("shard")
@@ -111,37 +109,20 @@
     offs = (0, 1, 3, 2)
     quarter = [mod4(z + off) for off in offs]
 
-    from_outer = [
-        [
+    def send_outer(i):
+        q = quarter[i]
+        return [
             push(src.at[c, q, :, theirs], buf.at[a, q, c, own_rows, :], outer)
             for a, src in enumerate((tok, grd))
         ]
-        for q in quarter
-    ]
+
+    from_outer = [send_outer(0)]
     own_tok = [
         bring(src.at[h, :, :, mine], buf.at[a, :, h, own_rows, :])
         for h in (0, 1)
         for a, src in enumerate((tok, grd))
     ]
     own_raw = [bring(gate_w, raw.at[0]), bring(up_w, raw.at[1]), bring(down_w, wt.at[2])]
-
-    for copy in own_tok:
-        copy.wait()
-    arrived(*from_outer[0])
-
-    def send_y(d):
-        at = {1: 2, 3: 1, 2: 3}[d] * 64
-        return push(buf.at[:, z, c, 0:64, :], buf.at[:, z, c, at : at + 64, :], along_y[d])
-
-    y_near = [send_y(1), send_y(3)]
-    y_far = send_y(2)
-
-    def outer_to_sibling(i):
-        ref = buf.at[:, quarter[i], c, outer_rows, :]
-        return push(ref, ref, sibling)
-
-    core_outer = [outer_to_sibling(0)]
-
     for copy in own_raw:
         copy.wait()
     for m in (0, 1):
@@ -152,32 +133,19 @@
         lax.fori_loop(0, 7, turn, 0)
     own_w = bring(wt.at[:, rows(Q * y, Q), :], wbuf.at[:, :, cols(y, B)])
 
-    def near(a, q):
-        return buf.at[a, q, c, 64:192, :]
-
-    def far(a, q):
-        return buf.at[a, q, c, 192:256, :]
-
-    both = slice(None)
-    core_piece = {}
-
-    def to_sibling(i, which, a=both):
-        ref = which(a, quarter[i])
-        core_piece.setdefault(i, []).append(push(ref, ref, sibling))
-
-    def spread(which):
-        ref = which(both, z)
-        return push(ref, ref, along_z[1]), push(ref, ref, along_z[3])
-
-    arrived(*y_near)
-    near_up, near_down = spread(near)
-    to_sibling(0, near)
-    for i in (1, 2, 3):
-        arrived(*from_outer[i])
-        core_outer.append(outer_to_sibling(i))
-    arrived(y_far)
-    far_up, far_down = spread(far)
-    to_sibling(0, far)
+    first, second = x_hi, 1 - x_hi
+    for copy in own_tok:
+        copy.wait()
+    arrived(*from_outer[0])
+
+    def send_y(d):
+        at = {1: 2, 3: 1, 2: 3}[d] * 64
+        return push(
+            buf.at[first, z, c, 0:64, :], buf.at[first, z, c, at : at + 64, :], along_y[d]
+        )
+
+    y_near = [send_y(1), send_y(3)]
+    y_far = send_y(2)
 
     def send_w(h):
         start, size = PARTS[h]
@@ -192,16 +160,57 @@
 
     from_w = [send_w(h) for h in range(len(PARTS))]
 
-    def onward(which, up, down):
+    def outer_to_sibling(i):
+        ref = buf.at[:, quarter[i], c, outer_rows, :]
+        return push(ref, ref, sibling)
+
+    core_outer = [outer_to_sibling(0)]
+
+    def near(a, q):
+        return buf.at[a, q, c, 64:192, :]
+
+    def far(a, q):
+        return buf.at[a, q, c, 192:256, :]
+
+    core_piece = {0: [], 1: [], 2: [], 3: []}
+
+    def to_sibling(i, which, a):
+        ref = which(a, quarter[i])
+        core_piece[i].append(push(ref, ref, sibling))
+
+    from_z = {}
+
+    def spread(which, a, name):
+        ref = which(a, z)
+        from_z[name] = push(ref, ref, along_z[1]), push(ref, ref, along_z[3])
+        to_sibling(0, which, a)
+
+    arrived(*y_near)
+    swap_near = push(near(first, z), near(first, z), across)
+    spread(near, first, "near 0")
+    arrived(y_far)
+    swap_far = push(far(first, z), far(first, z), across)
+    spread(far, first, "far 0")
+    from_outer += [send_outer(i) for i in (1, 2, 3)]
+    arrived(swap_near)
+    spread(near, second, "near 1")
+
+    onward = []
+
+    def relay(which, name):
+        up, down = from_z[name]
+        kind = 0 if name.endswith("0") else 1
+        a = second if kind else first
         arrived(up)
-        ref = which(0, quarter[2])
-        on_up = push(ref, ref, along_z[1])
-        to_sibling(2, which)
+        if kind == 0:
+            ref = which(a, quarter[2])
+            onward.append((push(ref, ref, along_z[1]), which, a))
+        to_sibling(2, which, a)
         arrived(down)
-        ref = which(1, quarter[1])
-        on_down = push(ref, ref, along_z[3])
-        to_sibling(1, which)
-        return on_up, on_down
+        if kind == 1:
+            ref = which(a, quarter[1])
+            onward.append((push(ref, ref, along_z[3]), which, a))
+        to_sibling(1, which, a)
 
     exchange = {}
 
@@ -358,26 +367,36 @@
                     lastsem.at[k, e - 1],
                 )
 
-    near_on = onward(near, near_up, near_down)
+    relay(near, "near 0")
+    arrived(swap_far)
+    spread(far, second, "far 1")
+    relay(far, "far 0")
     arrived(*core_outer, *core_piece[0])
     own_w.wait()
     arrived(*from_w[0])
     forward(0, 0)
-    far_on = onward(far, far_up, far_down)
-    arrived(*core_piece[1])
+    for i in (1, 2, 3):
+        arrived(*from_outer[i])
+        core_outer.append(outer_to_sibling(i))
+    relay(near, "near 1")
+    arrived(*from_w[1])
+    forward(0, 1)
+    activate(0, 0)
+    relay(far, "far 1")
+    weight_grads(0, 0)
+    arrived(*core_outer[1:], *core_piece[1])
     forward(1, 0)
     arrived(*core_piece[2])
     forward(2, 0)
-    arrived(*from_w[1])
-    forward(0, 1)
-    activate(0, 0)
-    weight_grads(0, 0)
-    arrived(*near_on)
-    to_sibling(3, near)
+    activate(0, 1)
+    token_grads(0)
+    weight_grads(0, 1)
+    along_z_grads(0)
+    for copy, which, a in onward:
+        arrived(copy)
+        to_sibling(3, which, a)
     activate(1, 0)
     weight_grads(1, 0)
-    arrived(*far_on)
-    to_sibling(3, far)
     arrived(*core_piece[3])
     forward(3, 0)
     forward(1, 1)
@@ -385,12 +404,8 @@
     forward(3, 1)
     activate(2, 0)
     weight_grads(2, 0)
-    activate(0, 1)
-    token_grads(0)
-    weight_grads(0, 1)
     activate(3, 0)
     last_weight_grads(3, 0)
-    along_z_grads(0)
     activate(1, 1)
     token_grads(1)
     weight_grads(1, 1)
@@ -415,8 +430,9 @@
             q = mod4(z - d + off)
             landed(zr.at[q, d - 1], zsem.at[q, d - 1])
     keep = z_rows(0)
-    from_yg = {}
-    for k, d in enumerate((1, 3, 2, 0)):
+    from_x, from_yg = [], {}
+
+    def over_x(k, d):
         at = cols(mod4(y + d), B)
         for e in (1, 2, 3):
             landed(zr.at[mod4(z - e + 2), e - 1, :, at], lastsem.at[k, e - 1])
@@ -426,9 +442,26 @@
             total = dxs[i, c, keep, at].astype(F32)
             for e in (0, 1, 2):
                 total = total + zr[q, e, :, at].astype(F32)
-            ys[q, :, at] = total.astype(BF16)
+            total = total.astype(BF16)
+            ys[0, q, :, at] = total[0:32]
+            ys[1, q, :, at] = total[32:64]
+        from_x.append(push(ys.at[1 - x_hi, :, :, at], xr.at[:, :, at], across))
+
+    def over_y(k, d):
+        at = cols(mod4(y + d), B)
+        arrived(from_x[k])
+        ys[x_hi, :, :, at] = (
+            ys[x_hi, :, :, at].astype(F32) + xr[:, :, at].astype(F32)
+        ).astype(BF16)
         if d:
-            from_yg[d] = push(ys.at[:, :, at], yr.at[d - 1], along_y[d])
+            from_yg[d] = push(ys.at[x_hi, :, :, at], yr.at[d - 1], along_y[d])
+
+    order = (1, 3, 2, 0)
+    over_x(0, order[0])
+    for k in (1, 2, 3):
+        over_x(k, order[k])
+        over_y(k - 1, order[k - 1])
+    over_y(3, order[3])
     for copy in own_dw:
         copy.wait()
     arrived(*from_dw[0], *from_dw[1])
@@ -438,17 +471,11 @@
             return carry
 
         lax.fori_loop(0, 7, turn, 0)
+    total = ys[x_hi, :, :, cols(y, B)].astype(F32)
     for d in (1, 3, 2):
         arrived(from_yg[d])
-    for q in range(4):
-        total = ys[q, :, cols(y, B)].astype(F32)
-        for d in (0, 1, 2):
-            total = total + yr[d, q].astype(F32)
-        xs[0, q] = total[0:32].astype(BF16)
-        xs[1, q] = total[32:64].astype(BF16)
-    from_x = push(xs.at[1 - x_hi], xr, across)
-    arrived(from_x)
-    dx[...] = (xs[x_hi].astype(F32) + xr[...].astype(F32)).astype(BF16).reshape(128, B)
+        total = total + yr[d - 1].astype(F32)
+    dx[...] = total.astype(BF16).reshape(128, B)
     left(*sent)
 
 
@@ -481,12 +508,11 @@
             pltpu.VMEM((4, 2, 256, DH), BF16),
             pltpu.VMEM((4, 256, DH), BF16),
             pltpu.VMEM((4, 3, 64, DH), BF16),
-            pltpu.VMEM((4, 64, DH), BF16),
-            pltpu.VMEM((3, 4, 64, B), BF16),
-            pltpu.VMEM((2, 4, 32, B), BF16),
-            pltpu.VMEM((4, 32, B), BF16),
-            pltpu.SemaphoreType.DMA((96,)),
-            pltpu.SemaphoreType.DMA((96,)),
+            pltpu.VMEM((2, 4, 32, DH), BF16),
+            pltpu.VMEM((4, 32, DH), BF16),
+            pltpu.VMEM((3, 4, 32, B), BF16),
+            pltpu.SemaphoreType.DMA((128,)),
+            pltpu.SemaphoreType.DMA((128,)),
             pltpu.SemaphoreType.DMA((16,)),
             pltpu.SemaphoreType.DMA((4, 3)),
             pltpu.SemaphoreType.DMA((4, 3)),

time: 172 us -> 167 us (0.971)
  Pallas kernels: 164 us -> 159 us
    pallas_call x1, Pallas kernels: 164 us -> 159 us  [local(): pl.pallas_call(kernel, out_shape=(jax.ShapeDtypeStruct((B, 4 * Q), BF16),...]
where the time goes in v3:
time: 167 us; the launch traced here: 166 us
  Pallas kernels  159 us (95%)
  other arithmetic  5.45 us (3%)
    pallas_call x1, Pallas kernels, local(): pl.pallas_call(kernel, out_shape=(jax.ShapeDtypeStruct((B, 4 * Q), BF16),...  159 us
    convert_element_type x3, other arithmetic, local(): return (dx, dgate.astype(F32), dup.astype(F32), ddown.astype(F32))  5.45 us

profile of v3, /device:TPU:0, one launch (start us, length us, event | category | flops | bytes accessed | tf_op | source)
XLA Modules:
  0.0 166.4 jit_solution(16056365324348434217)
XLA Ops:
  0.6 159.5 %shard_map.84 = (bf16[512,896]{1,0:T(8,128)(2,1)}, bf16[512,896]{1,0:T(8,128)(2,1)}, bf16[896,512]{1,0:T(8,128)(2,1)}, bf16[128,512]{1,0:T(8,128)(2,1)}) custom-call(bf16[2,4,32,4096]{3,2,1,0:T(8,128)(2,1)} %bitcast.2, bf16[2,4,32,4096]{3,2,1,0:T(8,128)(2,1)} %bitcast.3, bf16[512,896]{1,0:T(8,128)(2,1)} %gate_w.1, bf16[512,896]{1,0:T(8,128)(2,1)} %up_w.1, ...), custom_call_target="tpu_custom_call" | custom-call | flops 17179869184 | bytes 16777216 | tf_op jit(solution)/shard_map/pallas_call | solution.py:484
  160.1 0.0 copy-start.1
  160.1 2.6 %convert_element_type.9 = f32[512,896]{1,0:T(8,128)} convert(bf16[512,896]{1,0:T(8,128)(2,1)} %get-tuple-element.9) | non-fusion elementwise | flops 458752 | bytes 2752512 | tf_op jit(solution)/shard_map/convert_element_type | solution.py:528
  162.8 0.0 copy-done.1
  162.8 0.0 copy-start
  162.8 1.4 convert_element_type.10
  164.1 0.2 copy-done
  164.3 0.0 copy-start.2
  164.3 1.5 convert_element_type.11
  165.8 0.0 copy-done.2
  165.8 0.7 copy.10
Async XLA Ops:
  160.1 2.6 %copy-start.1 = (bf16[512,896]{1,0:T(8,128)(2,1)S(1)}, bf16[512,896]{1,0:T(8,128)(2,1)}, u32[]{:S(2)}) copy-start(bf16[512,896]{1,0:T(8,128)(2,1)} %get-tuple-element.10) | copy-start | bytes 2752516
  162.8 1.5 copy-start
  164.3 1.5 copy-start.2

commit v4 on v3

--- a/solution.py
+++ b/solution.py
@@ -123,6 +123,19 @@
         for a, src in enumerate((tok, grd))
     ]
     own_raw = [bring(gate_w, raw.at[0]), bring(up_w, raw.at[1]), bring(down_w, wt.at[2])]
+
+    first, second = x_hi, 1 - x_hi
+
+    def send_y(d, start):
+        at = rows({1: 2, 3: 1, 2: 3}[d] * 64 + start, 32)
+        return push(
+            buf.at[first, z, c, rows(start, 32), :], buf.at[first, z, c, at, :], along_y[d]
+        )
+
+    for copy in own_tok:
+        copy.wait()
+    y_near = [send_y(1, 32 * x_lo), send_y(3, 32 * x_lo)]
+    y_far = [send_y(2, 32 * x_lo)]
     for copy in own_raw:
         copy.wait()
     for m in (0, 1):
@@ -132,20 +145,9 @@
 
         lax.fori_loop(0, 7, turn, 0)
     own_w = bring(wt.at[:, rows(Q * y, Q), :], wbuf.at[:, :, cols(y, B)])
-
-    first, second = x_hi, 1 - x_hi
-    for copy in own_tok:
-        copy.wait()
     arrived(*from_outer[0])
-
-    def send_y(d):
-        at = {1: 2, 3: 1, 2: 3}[d] * 64
-        return push(
-            buf.at[first, z, c, 0:64, :], buf.at[first, z, c, at : at + 64, :], along_y[d]
-        )
-
-    y_near = [send_y(1), send_y(3)]
-    y_far = send_y(2)
+    y_near += [send_y(1, 32 * (1 - x_lo)), send_y(3, 32 * (1 - x_lo))]
+    y_far += [send_y(2, 32 * (1 - x_lo))]
 
     def send_w(h):
         start, size = PARTS[h]
@@ -188,7 +190,7 @@
     arrived(*y_near)
     swap_near = push(near(first, z), near(first, z), across)
     spread(near, first, "near 0")
-    arrived(y_far)
+    arrived(*y_far)
     swap_far = push(far(first, z), far(first, z), across)
     spread(far, first, "far 0")
     from_outer += [send_outer(i) for i in (1, 2, 3)]
@@ -367,9 +369,9 @@
                     lastsem.at[k, e - 1],
                 )
 
-    relay(near, "near 0")
     arrived(swap_far)
     spread(far, second, "far 1")
+    relay(near, "near 0")
     relay(far, "far 0")
     arrived(*core_outer, *core_piece[0])
     own_w.wait()
@@ -379,37 +381,37 @@
         arrived(*from_outer[i])
         core_outer.append(outer_to_sibling(i))
     relay(near, "near 1")
+    activate(0, 0)
+    weight_grads(0, 0)
     arrived(*from_w[1])
     forward(0, 1)
-    activate(0, 0)
     relay(far, "far 1")
-    weight_grads(0, 0)
     arrived(*core_outer[1:], *core_piece[1])
     forward(1, 0)
+    forward(1, 1)
     arrived(*core_piece[2])
     forward(2, 0)
     activate(0, 1)
     token_grads(0)
     weight_grads(0, 1)
     along_z_grads(0)
+    activate(1, 0)
+    weight_grads(1, 0)
     for copy, which, a in onward:
         arrived(copy)
         to_sibling(3, which, a)
-    activate(1, 0)
-    weight_grads(1, 0)
+    activate(1, 1)
+    token_grads(1)
     arrived(*core_piece[3])
     forward(3, 0)
-    forward(1, 1)
     forward(2, 1)
     forward(3, 1)
+    along_z_grads(1)
+    weight_grads(1, 1)
     activate(2, 0)
     weight_grads(2, 0)
     activate(3, 0)
     last_weight_grads(3, 0)
-    activate(1, 1)
-    token_grads(1)
-    weight_grads(1, 1)
-    along_z_grads(1)
     activate(2, 1)
     token_grads(2)
     weight_grads(2, 1)

time: 167 us -> 155 us (0.928)
  Pallas kernels: 159 us -> 147 us
    pallas_call x1, Pallas kernels: 159 us -> 147 us  [local(): pl.pallas_call(kernel, out_shape=(jax.ShapeDtypeStruct((B, 4 * Q), BF16),...]
where the time goes in v4:
time: 155 us; the launch traced here: 154 us
  Pallas kernels  147 us (95%)
  other arithmetic  5.45 us (4%)
    pallas_call x1, Pallas kernels, local(): pl.pallas_call(kernel, out_shape=(jax.ShapeDtypeStruct((B, 4 * Q), BF16),...  147 us
    convert_element_type x3, other arithmetic, local(): return (dx, dgate.astype(F32), dup.astype(F32), ddown.astype(F32))  5.45 us

profile of v4, /device:TPU:0, one launch (start us, length us, event | category | flops | bytes accessed | tf_op | source)
XLA Modules:
  0.0 154.0 jit_solution(12707225930331740944)
XLA Ops:
  0.6 147.1 %shard_map.84 = (bf16[512,896]{1,0:T(8,128)(2,1)}, bf16[512,896]{1,0:T(8,128)(2,1)}, bf16[896,512]{1,0:T(8,128)(2,1)}, bf16[128,512]{1,0:T(8,128)(2,1)}) custom-call(bf16[2,4,32,4096]{3,2,1,0:T(8,128)(2,1)} %bitcast.2, bf16[2,4,32,4096]{3,2,1,0:T(8,128)(2,1)} %bitcast.3, bf16[512,896]{1,0:T(8,128)(2,1)} %gate_w.1, bf16[512,896]{1,0:T(8,128)(2,1)} %up_w.1, ...), custom_call_target="tpu_custom_call" | custom-call | flops 17179869184 | bytes 16777216 | tf_op jit(solution)/shard_map/pallas_call | solution.py:486
  147.7 0.0 copy-start.1
  147.7 2.6 %convert_element_type.9 = f32[512,896]{1,0:T(8,128)} convert(bf16[512,896]{1,0:T(8,128)(2,1)} %get-tuple-element.9) | non-fusion elementwise | flops 458752 | bytes 2752512 | tf_op jit(solution)/shard_map/convert_element_type | solution.py:530
  150.3 0.0 copy-done.1
  150.3 0.0 copy-start
  150.3 1.4 convert_element_type.10
  151.7 0.2 copy-done
  151.8 0.0 copy-start.2
  151.8 1.5 convert_element_type.11
  153.3 0.0 copy-done.2
  153.3 0.7 copy.10
Async XLA Ops:
  147.7 2.6 %copy-start.1 = (bf16[512,896]{1,0:T(8,128)(2,1)S(1)}, bf16[512,896]{1,0:T(8,128)(2,1)}, u32[]{:S(2)}) copy-start(bf16[512,896]{1,0:T(8,128)(2,1)} %get-tuple-element.10) | copy-start | bytes 2752516
  150.3 1.5 copy-start
  151.8 1.5 copy-start.2

commit v5 on v4

--- a/solution.py
+++ b/solution.py
@@ -15,7 +15,7 @@
 DH = 2048
 B = 512
 CHUNK = 512
-PARTS = ((0, 128), (128, 96))
+PARTS = ((0, 80), (80, 80), (160, 64))
 
 
 def dot_nt(left, right):
@@ -31,8 +31,8 @@
 
 
 def kernel(
-    tok, grd, gate_w, up_w, down_w, dgate, dup, ddown, dx,
-    buf, raw, wt, wbuf, part, other, acc, back, dxs, dxr, zr, ys, xr, yr,
+    tok, grd, gate_w, up_w, down_w, back, ddown, dx,
+    buf, raw, wt, wbuf, part, other, acc, dxs, dxr, zr, ys, xr, yr,
     ssem, rsem, lsem, zsem, lastsem,
 ):
     grp, shard = lax.axis_index("grp"), lax.axis_index("shard")
@@ -372,53 +372,66 @@
     arrived(swap_far)
     spread(far, second, "far 1")
     relay(near, "near 0")
-    relay(far, "far 0")
     arrived(*core_outer, *core_piece[0])
     own_w.wait()
     arrived(*from_w[0])
     forward(0, 0)
+    relay(far, "far 0")
+    arrived(*from_w[1])
+    forward(0, 1)
     for i in (1, 2, 3):
         arrived(*from_outer[i])
         core_outer.append(outer_to_sibling(i))
-    relay(near, "near 1")
     activate(0, 0)
     weight_grads(0, 0)
-    arrived(*from_w[1])
-    forward(0, 1)
+    relay(near, "near 1")
+    activate(0, 1)
+    weight_grads(0, 1)
+    arrived(*from_w[2])
+    forward(0, 2)
     relay(far, "far 1")
     arrived(*core_outer[1:], *core_piece[1])
     forward(1, 0)
     forward(1, 1)
+    forward(1, 2)
+    activate(0, 2)
+    token_grads(0)
     arrived(*core_piece[2])
     forward(2, 0)
-    activate(0, 1)
-    token_grads(0)
-    weight_grads(0, 1)
+    forward(2, 1)
+    weight_grads(0, 2)
     along_z_grads(0)
     activate(1, 0)
     weight_grads(1, 0)
+    activate(1, 1)
+    weight_grads(1, 1)
     for copy, which, a in onward:
         arrived(copy)
         to_sibling(3, which, a)
-    activate(1, 1)
+    activate(1, 2)
     token_grads(1)
     arrived(*core_piece[3])
     forward(3, 0)
-    forward(2, 1)
+    forward(2, 2)
+    along_z_grads(1)
+    weight_grads(1, 2)
     forward(3, 1)
-    along_z_grads(1)
-    weight_grads(1, 1)
+    forward(3, 2)
     activate(2, 0)
     weight_grads(2, 0)
+    activate(2, 1)
+    weight_grads(2, 1)
     activate(3, 0)
     last_weight_grads(3, 0)
-    activate(2, 1)
+    activate(2, 2)
     token_grads(2)
-    weight_grads(2, 1)
+    weight_grads(2, 2)
     along_z_grads(2)
     activate(3, 1)
+    last_weight_grads(3, 1)
+    activate(3, 2)
     core_last = last_token_grads(3)
-    last_weight_grads(3, 1)
+    last_weight_grads(3, 2)
     last_along_z(3, core_last)
 
     def landed(ref, sem):
@@ -466,13 +479,8 @@
     over_y(3, order[3])
     for copy in own_dw:
         copy.wait()
-    arrived(*from_dw[0], *from_dw[1])
-    for m, out in enumerate((dgate, dup)):
-        def turn(n, carry):
-            out[:, cols(n, 128)] = back[m, cols(n, 128), :].T
-            return carry
-
-        lax.fori_loop(0, 7, turn, 0)
+    for h in range(len(PARTS)):
+        arrived(*from_dw[h])
     total = ys[x_hi, :, :, cols(y, B)].astype(F32)
     for d in (1, 3, 2):
         arrived(from_yg[d])
@@ -481,20 +489,24 @@
     left(*sent)
 
 
+def finish(back, down, dgate, dup, ddown):
+    dgate[...] = back[0].T.astype(F32)
+    dup[...] = back[1].T.astype(F32)
+    ddown[...] = down[...].astype(F32)
+
+
 def local(tokens, gate_weight, up_weight, down_weight, grad_out):
     flops = 8 * 2 * 2048 * 2048 * 256
-    dgate, dup, ddown, dx = pl.pallas_call(
+    back, ddown, dx = pl.pallas_call(
         kernel,
         out_shape=(
-            jax.ShapeDtypeStruct((B, 4 * Q), BF16),
-            jax.ShapeDtypeStruct((B, 4 * Q), BF16),
+            jax.ShapeDtypeStruct((2, 4 * Q, B), BF16),
             jax.ShapeDtypeStruct((4 * Q, B), BF16),
             jax.ShapeDtypeStruct((128, B), BF16),
         ),
         in_specs=[pl.BlockSpec(memory_space=pl.ANY)] * 5,
         out_specs=(
-            pl.BlockSpec(memory_space=pltpu.VMEM),
-            pl.BlockSpec(memory_space=pltpu.VMEM),
+            pl.BlockSpec(memory_space=pl.ANY),
             pl.BlockSpec(memory_space=pl.ANY),
             pl.BlockSpec(memory_space=pltpu.VMEM),
         ),
@@ -506,7 +518,6 @@
             pltpu.VMEM((4, 3, Q, CHUNK), BF16),
             pltpu.VMEM((4, 3, Q, CHUNK), BF16),
             pltpu.VMEM((3, Q, DH), F32),
-            pltpu.VMEM((2, 4 * Q, B), BF16),
             pltpu.VMEM((4, 2, 256, DH), BF16),
             pltpu.VMEM((4, 256, DH), BF16),
             pltpu.VMEM((4, 3, 64, DH), BF16),
@@ -527,7 +538,26 @@
         tokens.reshape(2, 4, 32, 4096), grad_out.reshape(2, 4, 32, 4096),
         gate_weight, up_weight, down_weight,
     )
-    return (dx, dgate.astype(F32), dup.astype(F32), ddown.astype(F32))
+    grads = pl.pallas_call(
+        finish,
+        grid=(7,),
+        out_shape=(
+            jax.ShapeDtypeStruct((B, 4 * Q), F32),
+            jax.ShapeDtypeStruct((B, 4 * Q), F32),
+            jax.ShapeDtypeStruct((4 * Q, B), F32),
+        ),
+        in_specs=[
+            pl.BlockSpec((2, 128, B), lambda n: (0, n, 0)),
+            pl.BlockSpec((128, B), lambda n: (n, 0)),
+        ],
+        out_specs=(
+            pl.BlockSpec((B, 128), lambda n: (0, n)),
+            pl.BlockSpec((B, 128), lambda n: (0, n)),
+            pl.BlockSpec((128, B), lambda n: (n, 0)),
+        ),
+        cost_estimate=pl.CostEstimate(flops=0, bytes_accessed=2**23, transcendentals=0),
+    )(back, ddown)
+    return (dx, *grads)
 
 
 def solution(mesh):

time: 155 us -> 150 us (0.968)
  other arithmetic: 5.45 us -> 0 us
    convert_element_type x3 -> x0, other arithmetic: 5.45 us -> none  [local(): return (dx, dgate.astype(F32), dup.astype(F32), ddown.astype(F32))]
    pallas_call x1 -> x2, Pallas kernels: 147 us -> 148 us  [the longest x1 142 us: local(): pl.pallas_call(kernel, out_shape=(jax.ShapeDtypeStruct((2, 4 * Q, B), BF1...]
where the time goes in v5:
time: 150 us; the launch traced here: 149 us
  Pallas kernels  148 us (99%)
    pallas_call x1, Pallas kernels, local(): pl.pallas_call(kernel, out_shape=(jax.ShapeDtypeStruct((2, 4 * Q, B), BF1...  142 us
    pallas_call x1, Pallas kernels, local(): pl.pallas_call(finish, grid=(7,), out_shape=(jax.ShapeDtypeStruct((B, 4 *...  6.27 us

profile of v5, /device:TPU:0, one launch (start us, length us, event | category | flops | bytes accessed | tf_op | source)
XLA Modules:
  0.0 149.4 jit_solution(12954621504568309563)
XLA Ops:
  0.6 141.8 %shard_map.84 = (bf16[2,896,512]{2,1,0:T(8,128)(2,1)}, bf16[896,512]{1,0:T(8,128)(2,1)}, bf16[128,512]{1,0:T(8,128)(2,1)}) custom-call(bf16[2,4,32,4096]{3,2,1,0:T(8,128)(2,1)} %bitcast.2, bf16[2,4,32,4096]{3,2,1,0:T(8,128)(2,1)} %bitcast.3, bf16[512,896]{1,0:T(8,128)(2,1)} %gate_w.1, bf16[512,896]{1,0:T(8,128)(2,1)} %up_w.1, bf16[896,512]{1,0:T(8,128)(2,1)} %down_w.1), custom_call_target="tpu_custom_call" | custom-call | flops 17179869184 | bytes 16777216 | tf_op jit(solution)/shard_map/pallas_call | solution.py:500
  142.5 0.0 copy-start
  142.5 6.3 %shard_map.85 = (f32[512,896]{1,0:T(8,128)}, f32[512,896]{1,0:T(8,128)}, f32[896,512]{1,0:T(8,128)}) custom-call(bf16[2,896,512]{2,1,0:T(8,128)(2,1)} %get-tuple-element.11.back, bf16[896,512]{1,0:T(8,128)(2,1)} %get-tuple-element.12.down), custom_call_target="tpu_custom_call" | custom-call | bytes 8388608 | tf_op jit(solution)/shard_map/pallas_call | solution.py:541
  148.8 0.0 copy-done
  148.8 0.7 copy.10
Async XLA Ops:
  142.5 6.3 %copy-start = (bf16[128,512]{1,0:T(8,128)(2,1)S(1)}, bf16[128,512]{1,0:T(8,128)(2,1)}, u32[]{:S(2)}) copy-start(bf16[128,512]{1,0:T(8,128)(2,1)} %get-tuple-element.20) | copy-start | bytes 393220

commit v6 on v5

v6 whole, which is shorter than its diff:
```python
import functools

import jax
import jax.numpy as jnp
from jax import lax
from jax.experimental import pallas as pl
from jax.experimental.pallas import tpu as pltpu
from jax.sharding import PartitionSpec as P

MESH = pl.DeviceIdType.MESH
BF16 = jnp.bfloat16
F32 = jnp.float32

Q = 224
DH = 2048
B = 512
CHUNK = 512
H0, H1, H2 = PARTS = ((0, 80), (80, 80), (160, 64))
H01, H12, ALL = (0, 160), (80, 144), (0, Q)


def dot_nt(left, right):
    return lax.dot_general(left, right, (((1,), (1,)), ((), ())), preferred_element_type=F32)


def dot_nn(left, right):
    return lax.dot_general(left, right, (((1,), (0,)), ((), ())), preferred_element_type=F32)


def dot_tn(left, right):
    return lax.dot_general(left, right, (((0,), (0,)), ((), ())), preferred_element_type=F32)


def kernel(
    tok, grd, gate_w, up_w, down_w, back, ddown, dx,
    buf, raw, wt, wbuf, part, other, acc, dxs, dxr, zr, ys, xr, yr, yf, zs, zy,
    ssem, rsem, lsem, zsem, lastsem,
):
    grp, shard = lax.axis_index("grp"), lax.axis_index("shard")
    x_lo, y = lax.div(grp, 4), lax.rem(grp, 4)
    x_hi, z, c = lax.div(shard, 8), lax.rem(lax.div(shard, 2), 4), lax.rem(shard, 2)
    x = 2 * x_hi + x_lo

    def mod4(v):
        return lax.rem(v + 8, 4)

    def slot(dy):
        return dy + lax.div(dy, 2) * (1 - 2 * lax.rem(dy, 2))

    def device(x, y, z, c):
        return (4 * lax.rem(x, 2) + y, 8 * lax.div(x, 2) + 2 * z + c)

    sibling = device(x, y, z, 1 - c)
    inner = device(x + 1 - 2 * x_lo, y, z, c)
    outer = device(mod4(x - 1 + 2 * x_lo), y, z, c)
    across = device(mod4(x + 2), y, z, c)
    along_y = {d: device(x, mod4(y + d), z, c) for d in (1, 2, 3)}
    along_z = {d: device(x, y, mod4(z + d), c) for d in (1, 2, 3)}

    barrier = pltpu.get_barrier_semaphore()
    partners = [sibling, inner, outer, across, *along_y.values(), *along_z.values()]
    for partner in partners:
        pl.semaphore_signal(barrier, inc=1, device_id=partner, device_id_type=MESH)

    count = [0]
    sent = []

    def push(src, dst, target, recv=None):
        n = count[0]
        count[0] += 1
        copy = pltpu.make_async_remote_copy(
            src_ref=src, dst_ref=dst, send_sem=ssem.at[n],
            recv_sem=rsem.at[n] if recv is None else recv,
            device_id=target, device_id_type=MESH,
        )
        copy.start()
        sent.append(copy)
        return copy

    local_count = [0]

    def bring(src, dst):
        n = local_count[0]
        local_count[0] += 1
        copy = pltpu.make_async_copy(src, dst, lsem.at[n])
        copy.start()
        return copy

    def arrived(*copies):
        for copy in copies:
            copy.wait_recv()

    gone = set()

    def left(*copies):
        for copy in copies:
            if id(copy) not in gone:
                gone.add(id(copy))
                copy.wait_send()

    def rows(start, size, step=32):
        return pl.ds(pl.multiple_of(start, step), size)

    def cols(block, size):
        return pl.ds(pl.multiple_of(block * size, size), size)

    mine, theirs = cols(x_lo, DH), cols(1 - x_lo, DH)
    own_rows, outer_rows = rows(16 * x_lo, 16, 16), rows(16 * (1 - x_lo), 16, 16)
    offs = (0, 1, 3, 2)
    quarter = [mod4(z + off) for off in offs]
    first, second = x_hi, 1 - x_hi

    def half(u):
        return first + u * (1 - 2 * first)

    own_tok = [
        bring(src.at[h, :, s, :, mine], buf.at[a, :, s, h, own_rows, :])
        for s in (0, 1)
        for h in (0, 1)
        for a, src in enumerate((tok, grd))
    ]
    own_raw = [bring(gate_w, raw.at[0]), bring(up_w, raw.at[1]), bring(down_w, wt.at[2])]
    for copy in own_raw:
        copy.wait()
    for m in (0, 1):
        def turn(n, carry):
            wt[m, cols(n, 128), :] = raw[m, :, cols(n, 128)].T
            return carry

        lax.fori_loop(0, 7, turn, 0)
    own_w = bring(wt.at[:, rows(Q * y, Q), :], wbuf.at[:, :, cols(y, B)])
    for copy in own_tok:
        copy.wait()
    pl.semaphore_wait(barrier, len(partners))

    def send_outer(i, target):
        q = quarter[i]
        return [
            push(src.at[c, q, :, :, theirs], buf.at[a, q, :, c, own_rows, :], target)
            for a, src in enumerate((tok, grd))
        ]

    from_outer = {0: send_outer(0, outer), 2: send_outer(2, inner), 1: send_outer(1, outer)}

    def send_y(d, lo):
        src = rows(16 * lo, 16, 16)
        dst = rows({1: 2, 3: 1, 2: 3}[d] * 32 + 16 * lo, 16, 16)
        return push(buf.at[:, z, first, c, src, :], buf.at[:, z, first, c, dst, :], along_y[d])

    y_near = [send_y(1, x_lo), send_y(3, x_lo)]
    y_far = [send_y(2, x_lo)]
    arrived(*from_outer[0])
    y_near += [send_y(1, 1 - x_lo), send_y(3, 1 - x_lo)]
    y_far += [send_y(2, 1 - x_lo)]

    def send_w(h):
        start, size = PARTS[h]
        return [
            push(
                wt.at[:, rows(Q * mod4(y + d) + start, size, 16), :],
                wbuf.at[:, start : start + size, cols(y, B)],
                along_y[d],
            )
            for d in (1, 3, 2)
        ]

    from_w = [send_w(h) for h in range(len(PARTS))]

    def outer_to_sibling(i):
        ref = buf.at[:, quarter[i], :, c, outer_rows, :]
        return push(ref, ref, sibling)

    core_outer = [outer_to_sibling(0)]

    def near(s, q):
        return buf.at[:, q, s, c, 32:96, :]

    def far(s, q):
        return buf.at[:, q, s, c, 96:128, :]

    core_piece = {(i, u): [] for i in range(4) for u in (0, 1)}

    def to_sibling(i, u, which):
        ref = which(half(u), quarter[i])
        core_piece[i, u].append(push(ref, ref, sibling))

    from_z = {}

    def spread(which, u):
        ref = which(half(u), z)
        from_z[which, u] = push(ref, ref, along_z[1]), push(ref, ref, along_z[3])
        to_sibling(0, u, which)

    arrived(*y_near)
    swap_near = push(near(first, z), near(first, z), across)
    spread(near, 0)
    arrived(*y_far)
    swap_far = push(far(first, z), far(first, z), across)
    spread(far, 0)
    from_outer[3] = send_outer(3, outer)
    arrived(swap_near)
    spread(near, 1)

    onward = []

    def relay(which, u):
        up, down = from_z[which, u]
        arrived(up)
        if u == 0:
            ref = which(half(u), quarter[2])
            onward.append((push(ref, ref, along_z[1]), which, u))
        to_sibling(2, u, which)
        arrived(down)
        if u == 1:
            ref = which(half(u), quarter[1])
            onward.append((push(ref, ref, along_z[3]), which, u))
        to_sibling(1, u, which)

    exchange = {}

    def forward(i, us, span):
        q = quarter[i]
        start, size = span
        hidden = slice(start, start + size)

        def one(u, carry):
            s = half(u)
            part[i, u, 0:2, hidden, :] = dot_nt(
                wbuf[0:2, hidden, :].reshape(2 * size, DH), buf[0, q, s].reshape(256, DH)
            ).astype(BF16).reshape(2, size, 256)
            part[i, u, 2, hidden, :] = dot_nt(
                wbuf[2, hidden, :], buf[1, q, s].reshape(256, DH)
            ).astype(BF16)
            return carry

        lax.fori_loop(us[0], us[-1] + 1, one, 0)
        at = slice(us[0], us[-1] + 1)
        exchange[i, us, span] = push(
            part.at[i, at, :, hidden, :], other.at[i, at, :, hidden, :], inner
        )

    def activate(i, us, span):
        arrived(exchange[i, us, span])
        left(exchange[i, us, span])
        start, size = span
        pair = slice(us[0], us[-1] + 1)
        step = 16 if len(us) == 2 or size % 32 else 32

        def some(r, carry):
            at = rows(start + step * r, step, 16)

            def full(m):
                return part[i, pair, m, at, :].astype(F32) + other[i, pair, m, at, :].astype(F32)

            gate, up_pre, back_grad = full(0), full(1), full(2)
            s = jax.nn.sigmoid(gate)
            silu = gate * s
            part[i, pair, 0, at, :] = (
                back_grad * up_pre * s * (1.0 + gate * (1.0 - s))
            ).astype(BF16)
            part[i, pair, 1, at, :] = (back_grad * silu).astype(BF16)
            part[i, pair, 2, at, :] = (silu * up_pre).astype(BF16)
            return carry

        lax.fori_loop(0, size // step, some, 0)

    def weight_terms(i, span, n):
        q = quarter[i]
        start, size = span
        hidden = slice(start, start + size)
        at = cols(n, B)
        pair, third = 0.0, 0.0
        for u in (0, 1):
            pair = pair + dot_nn(
                part[i, u, 0:2, hidden, :].reshape(2 * size, 256),
                buf[0, q, half(u), :, :, at].reshape(256, B),
            )
            third = third + dot_nn(
                part[i, u, 2, hidden, :], buf[1, q, half(u), :, :, at].reshape(256, B)
            )
        return pair.reshape(2, size, B), third

    def weight_grads(i, span):
        start, size = span
        hidden = slice(start, start + size)

        def block(n, carry):
            pair, third = weight_terms(i, span, n)
            at = cols(n, B)
            if i:
                pair = pair + acc[0:2, hidden, at]
                third = third + acc[2, hidden, at]
            acc[0:2, hidden, at] = pair
            acc[2, hidden, at] = third
            return carry

        lax.fori_loop(0, 4, block, 0)

    from_dw, own_dw = {}, []

    def last_weight_grads(i, span):
        if span == H0:
            for copies in from_w:
                for copy in copies:
                    left(copy)
        start, size = span
        hidden = slice(start, start + size)
        from_dw[span] = []
        for d in (1, 3, 2, 0):
            n = mod4(y + d)
            pair, third = weight_terms(i, span, n)
            at = cols(n, B)
            held = rows(Q * n + start, size, 16)
            wt[0:2, held, :] = (pair + acc[0:2, hidden, at]).astype(BF16)
            wt[2, held, :] = (third + acc[2, hidden, at]).astype(BF16)
            there = rows(Q * y + start, size, 16)
            if d:
                from_dw[span].append(push(wt.at[0:2, held, :], back.at[:, there, :], along_y[d]))
                from_dw[span].append(push(wt.at[2, held, :], ddown.at[there, :], along_y[d]))
            else:
                own_dw.append(bring(wt.at[0:2, held, :], back.at[:, there, :]))
                own_dw.append(bring(wt.at[2, held, :], ddown.at[there, :]))

    def turned(i, u):
        return part[i, u, 0:2].reshape(2 * Q, 256).T

    def token_terms(i, u, n, deltas):
        at = cols(n, B)
        dxs[i, u, :, :, at] = dot_nn(
            deltas, wbuf[0:2, :, at].reshape(2 * Q, B)
        ).astype(BF16).reshape(2, 128, B)

    core_dx = {}

    def token_grads(i, us):
        for u in us:
            deltas = turned(i, u)

            def block(n, carry):
                token_terms(i, u, n, deltas)
                return carry

            lax.fori_loop(0, 4, block, 0)
            core_dx[i, u] = push(dxs.at[i, u, 1 - c], dxr.at[i, u], sibling)

    def add_core(i, u, at):
        dxs[i, u, c, :, at] = (
            dxs[i, u, c, :, at].astype(F32) + dxr[i, u, :, at].astype(F32)
        ).astype(BF16)

    def add_core_whole(i, u):
        arrived(core_dx[i, u])

        def some(n, carry):
            add_core(i, u, cols(n, B))
            return carry

        lax.fori_loop(0, 4, some, 0)

    def block_rows(yb):
        return rows(32 * slot(mod4(yb)), 32)

    def along_z_grads(i, us):
        q = quarter[i]
        for u in us:
            add_core_whole(i, u)
            for d in (1, 3, 2):
                push(
                    dxs.at[i, u, c, block_rows(z + d - y), :], zr.at[q, u, d - 1], along_z[d],
                    zsem.at[q, u, d - 1],
                )

    from_yf, from_zy = {}, {}

    def along_y_grads():
        for u in (0, 1):
            add_core_whole(0, u)
        for d in (1, 3, 2):
            at = cols(mod4(y + d), B)
            from_yf[d] = push(dxs.at[0, :, c, :, at], yf.at[d - 1], along_y[d])

    def then_along_z():
        for d in (1, 3, 2):
            arrived(from_yf[d])
        for e in (1, 3, 2, 0):
            total = dxs[0, :, c, block_rows(z + e - y), cols(y, B)].astype(F32)
            for d in (1, 2, 3):
                total = total + yf[d - 1, :, block_rows(z + e - y + d), :].astype(F32)
            zs[e] = total.astype(BF16)
            if e:
                from_zy[e] = push(zs.at[e], zy.at[e - 1], along_z[e])

    def last_token_grads():
        core_last = {}
        deltas = turned(3, 1)
        for d in (1, 3, 2, 0):
            n = mod4(y + d)
            token_terms(3, 1, n, deltas)
            at = cols(n, B)
            core_last[d] = push(dxs.at[3, 1, 1 - c, :, at], dxr.at[3, 1, :, at], sibling)
        return core_last

    def last_along_z(core_last):
        for k, d in enumerate((1, 3, 2, 0)):
            at = cols(mod4(y + d), B)
            arrived(core_last[d])
            add_core(3, 1, at)
            for e in (1, 3, 2):
                push(
                    dxs.at[3, 1, c, block_rows(z + e - y), at],
                    zr.at[quarter[3], 1, e - 1, :, at], along_z[e], lastsem.at[k, e - 1],
                )

    whole, one, two = (0, 1), (0,), (1,)
    arrived(swap_far)
    spread(far, 1)
    relay(near, 0)
    arrived(*core_outer, *core_piece[0, 0], *core_piece[0, 1])
    own_w.wait()
    arrived(*from_w[0])
    forward(0, whole, H0)
    relay(far, 0)
    arrived(*from_w[1])
    forward(0, whole, H1)
    for i in (1, 2):
        arrived(*from_outer[i])
        core_outer.append(outer_to_sibling(i))
    arrived(*core_outer[1:], *core_piece[1, 0], *core_piece[2, 0])
    forward(1, one, H01)
    forward(2, one, H01)
    activate(0, whole, H0)
    relay(near, 1)
    activate(0, whole, H1)
    arrived(*from_w[2])
    forward(0, whole, H2)
    forward(1, one, H2)
    forward(2, one, H2)
    relay(far, 1)
    arrived(*core_piece[1, 1])
    forward(1, two, ALL)
    activate(1, one, H01)
    activate(2, one, H01)
    arrived(*core_piece[2, 1])
    forward(2, two, H0)
    activate(0, whole, H2)
    token_grads(0, whole)
    weight_grads(0, ALL)
    along_y_grads()
    activate(1, one, H2)
    token_grads(1, one)
    activate(2, one, H2)
    token_grads(2, one)
    along_z_grads(1, one)
    for copy, which, u in onward:
        arrived(copy)
        to_sibling(3, u, which)
    arrived(*from_outer[3])
    core_outer.append(outer_to_sibling(3))
    along_z_grads(2, one)
    activate(1, two, ALL)
    token_grads(1, two)
    arrived(core_outer[3], *core_piece[3, 0], *core_piece[3, 1])
    forward(3, whole, H0)
    forward(2, two, H12)
    along_z_grads(1, two)
    forward(3, whole, H1)
    weight_grads(1, ALL)
    activate(2, two, H0)
    weight_grads(2, H0)
    then_along_z()
    forward(3, one, H2)
    forward(3, two, H2)
    activate(3, whole, H0)
    last_weight_grads(3, H0)
    activate(2, two, H12)
    token_grads(2, two)
    weight_grads(2, H12)
    along_z_grads(2, two)
    activate(3, whole, H1)
    last_weight_grads(3, H1)
    activate(3, one, H2)
    token_grads(3, one)
    activate(3, two, H2)
    core_last = last_token_grads()
    last_weight_grads(3, H2)
    along_z_grads(3, one)
    last_along_z(core_last)

    def landed(ref, sem):
        pltpu.make_async_remote_copy(
            src_ref=ref, dst_ref=ref, send_sem=ssem.at[0], recv_sem=sem,
            device_id=along_z[1], device_id_type=MESH,
        ).wait_recv()

    for d in (1, 2, 3):
        for i, u in ((1, 0), (1, 1), (2, 0), (2, 1), (3, 0)):
            q = mod4(z - d + offs[i])
            landed(zr.at[q, u, d - 1], zsem.at[q, u, d - 1])
    keep = block_rows(z - y)
    from_x, from_yg = [], {}

    def over_x(k, d):
        at = cols(mod4(y + d), B)
        for e in (1, 2, 3):
            landed(zr.at[mod4(z - e + 2), 1, e - 1, :, at], lastsem.at[k, e - 1])

        for i in range(4):
            q = quarter[i]
            for u in (0, 1):
                terms = [zr[q, u, e - 1, :, at] for e in (1, 2, 3) if (offs[i] + e) % 4]
                if i:
                    terms.append(dxs[i, u, c, keep, at])
                if d == 0:
                    terms.append(zy[3 - offs[i], u] if i else zs[0, u])
                total = sum(term.astype(F32) for term in terms).astype(BF16)
                ys[0, q, half(u), :, at] = total[0:16]
                ys[1, q, half(u), :, at] = total[16:32]
        from_x.append(push(ys.at[1 - x_hi, :, :, :, at], xr.at[:, :, :, at], across))

    def over_y(k, d):
        at = cols(mod4(y + d), B)
        arrived(from_x[k])
        ys[x_hi, :, :, :, at] = (
            ys[x_hi, :, :, :, at].astype(F32) + xr[:, :, :, at].astype(F32)
        ).astype(BF16)
        if d:
            from_yg[d] = push(ys.at[x_hi, :, :, :, at], yr.at[d - 1], along_y[d])

    order = (1, 3, 2, 0)
    arrived(*from_zy.values())
    over_x(0, order[0])
    for k in (1, 2, 3):
        over_x(k, order[k])
        over_y(k - 1, order[k - 1])
    over_y(3, order[3])
    for copy in own_dw:
        copy.wait()
    for span in PARTS:
        arrived(*from_dw[span])
    total = ys[x_hi, :, :, :, cols(y, B)].astype(F32)
    for d in (1, 3, 2):
        arrived(from_yg[d])
        total = total + yr[d - 1].astype(F32)
    dx[...] = total.astype(BF16).reshape(128, B)
    left(*sent)


def finish(back, down, dgate, dup, ddown):
    dgate[...] = back[0].T.astype(F32)
    dup[...] = back[1].T.astype(F32)
    ddown[...] = down[...].astype(F32)


def local(tokens, gate_weight, up_weight, down_weight, grad_out):
    flops = 8 * 2 * 2048 * 2048 * 256
    back, ddown, dx = pl.pallas_call(
        kernel,
        out_shape=(
            jax.ShapeDtypeStruct((2, 4 * Q, B), BF16),
            jax.ShapeDtypeStruct((4 * Q, B), BF16),
            jax.ShapeDtypeStruct((128, B), BF16),
        ),
        in_specs=[pl.BlockSpec(memory_space=pl.ANY)] * 5,
        out_specs=(
            pl.BlockSpec(memory_space=pl.ANY),
            pl.BlockSpec(memory_space=pl.ANY),
            pl.BlockSpec(memory_space=pltpu.VMEM),
        ),
        scratch_shapes=[
            pltpu.VMEM((2, 4, 2, 2, 128, DH), BF16),
            pltpu.VMEM((2, B, 4 * Q), BF16),
            pltpu.VMEM((3, 4 * Q, B), BF16),
            pltpu.VMEM((3, Q, DH), BF16),
            pltpu.VMEM((4, 2, 3, Q, 256), BF16),
            pltpu.VMEM((4, 2, 3, Q, 256), BF16),
            pltpu.VMEM((3, Q, DH), F32),
            pltpu.VMEM((4, 2, 2, 128, DH), BF16),
            pltpu.VMEM((4, 2, 128, DH), BF16),
            pltpu.VMEM((4, 2, 3, 32, DH), BF16),
            pltpu.VMEM((2, 4, 2, 16, DH), BF16),
            pltpu.VMEM((4, 2, 16, DH), BF16),
            pltpu.VMEM((3, 4, 2, 16, B), BF16),
            pltpu.VMEM((3, 2, 128, B), BF16),
            pltpu.VMEM((4, 2, 32, B), BF16),
            pltpu.VMEM((3, 2, 32, B), BF16),
            pltpu.SemaphoreType.DMA((160,)),
            pltpu.SemaphoreType.DMA((160,)),
            pltpu.SemaphoreType.DMA((24,)),
            pltpu.SemaphoreType.DMA((4, 2, 3)),
            pltpu.SemaphoreType.DMA((4, 3)),
        ],
        compiler_params=pltpu.CompilerParams(
            collective_id=0, has_side_effects=True, vmem_limit_bytes=62 * 2**20
        ),
        cost_estimate=pl.CostEstimate(flops=flops, bytes_accessed=2**24, transcendentals=2**20),
    )(
        tokens.reshape(2, 4, 2, 16, 4096), grad_out.reshape(2, 4, 2, 16, 4096),
        gate_weight, up_weight, down_weight,
    )
    grads = pl.pallas_call(
        finish,
        grid=(7,),
        out_shape=(
            jax.ShapeDtypeStruct((B, 4 * Q), F32),
            jax.ShapeDtypeStruct((B, 4 * Q), F32),
            jax.ShapeDtypeStruct((4 * Q, B), F32),
        ),
        in_specs=[
            pl.BlockSpec((2, 128, B), lambda n: (0, n, 0)),
            pl.BlockSpec((128, B), lambda n: (n, 0)),
        ],
        out_specs=(
            pl.BlockSpec((B, 128), lambda n: (0, n)),
            pl.BlockSpec((B, 128), lambda n: (0, n)),
            pl.BlockSpec((128, B), lambda n: (n, 0)),
        ),
        cost_estimate=pl.CostEstimate(flops=0, bytes_accessed=2**23, transcendentals=0),
    )(back, ddown)
    return (dx, *grads)


def solution(mesh):
    return jax.shard_map(
        local,
        mesh=mesh,
        in_specs=(
            P("grp", None),
            P("grp", "shard"),
            P("grp", "shard"),
            P("shard", "grp"),
            P("grp", None),
        ),
        out_specs=(P("shard", "grp"), P("grp", "shard"), P("grp", "shard"), P("shard", "grp")),
        check_vma=False,
    )
```

time: 150 us -> 146 us (0.973)
  Pallas kernels: 148 us -> 144 us
    pallas_call x1, Pallas kernels: 142 us -> 138 us  [local(): pl.pallas_call(kernel, out_shape=(jax.ShapeDtypeStruct((2, 4 * Q, B), BF1...]
where the time goes in v6:
time: 146 us; the launch traced here: 145 us
  Pallas kernels  144 us (99%)
    pallas_call x1, Pallas kernels, local(): pl.pallas_call(kernel, out_shape=(jax.ShapeDtypeStruct((2, 4 * Q, B), BF1...  138 us
    pallas_call x1, Pallas kernels, local(): pl.pallas_call(finish, grid=(7,), out_shape=(jax.ShapeDtypeStruct((B, 4 *...  6.27 us

profile of v6, /device:TPU:0, one launch (start us, length us, event | category | flops | bytes accessed | tf_op | source)
XLA Modules:
  0.0 145.4 jit_solution(4231923190370795728)
XLA Ops:
  0.6 137.8 %shard_map.84 = (bf16[2,896,512]{2,1,0:T(8,128)(2,1)}, bf16[896,512]{1,0:T(8,128)(2,1)}, bf16[128,512]{1,0:T(8,128)(2,1)}) custom-call(bf16[2,4,2,16,4096]{4,3,2,1,0:T(8,128)(2,1)} %bitcast.2, bf16[2,4,2,16,4096]{4,3,2,1,0:T(8,128)(2,1)} %bitcast.3, bf16[512,896]{1,0:T(8,128)(2,1)} %gate_w.1, bf16[512,896]{1,0:T(8,128)(2,1)} %up_w.1, bf16[896,512]{1,0:T(8,128)(2,1)} %down_w.1), custom_call_target="tpu_custom_call" | custom-call | flops 17179869184 | bytes 16777216 | tf_op jit(solution)/shard_map/pallas_call | solution.py:556
  138.5 0.0 copy-start
  138.5 6.3 %shard_map.85 = (f32[512,896]{1,0:T(8,128)}, f32[512,896]{1,0:T(8,128)}, f32[896,512]{1,0:T(8,128)}) custom-call(bf16[2,896,512]{2,1,0:T(8,128)(2,1)} %get-tuple-element.11.back, bf16[896,512]{1,0:T(8,128)(2,1)} %get-tuple-element.12.down), custom_call_target="tpu_custom_call" | custom-call | bytes 8388608 | tf_op jit(solution)/shard_map/pallas_call | solution.py:600
  144.7 0.0 copy-done
  144.7 0.7 copy.10
Async XLA Ops:
  138.5 6.3 %copy-start = (bf16[128,512]{1,0:T(8,128)(2,1)S(1)}, bf16[128,512]{1,0:T(8,128)(2,1)}, u32[]{:S(2)}) copy-start(bf16[128,512]{1,0:T(8,128)(2,1)} %get-tuple-element.20) | copy-start | bytes 393220

commit v7 on v6

--- a/solution.py
+++ b/solution.py
@@ -15,8 +15,9 @@
 DH = 2048
 B = 512
 CHUNK = 512
-H0, H1, H2 = PARTS = ((0, 80), (80, 80), (160, 64))
-H01, H12, ALL = (0, 160), (80, 144), (0, Q)
+H0, H1, H2 = COME = ((0, 80), (80, 80), (160, 64))
+D0, D1, D2 = GO = ((0, 96), (96, 64), (160, 64))
+H01, H12, D12, ALL = (0, 160), (80, 144), (96, 128), (0, Q)
 
 
 def dot_nt(left, right):
@@ -105,7 +106,6 @@
         return pl.ds(pl.multiple_of(block * size, size), size)
 
     mine, theirs = cols(x_lo, DH), cols(1 - x_lo, DH)
-    own_rows, outer_rows = rows(16 * x_lo, 16, 16), rows(16 * (1 - x_lo), 16, 16)
     offs = (0, 1, 3, 2)
     quarter = [mod4(z + off) for off in offs]
     first, second = x_hi, 1 - x_hi
@@ -114,7 +114,7 @@
         return first + u * (1 - 2 * first)
 
     own_tok = [
-        bring(src.at[h, :, s, :, mine], buf.at[a, :, s, h, own_rows, :])
+        bring(src.at[h, :, s, :, mine], buf.at[a, :, s, h, 0, x_lo])
         for s in (0, 1)
         for h in (0, 1)
         for a, src in enumerate((tok, grd))
@@ -136,25 +136,54 @@
     def send_outer(i, target):
         q = quarter[i]
         return [
-            push(src.at[c, q, :, :, theirs], buf.at[a, q, :, c, own_rows, :], target)
+            push(src.at[c, q, :, :, theirs], buf.at[a, q, :, c, 0, x_lo], target)
             for a, src in enumerate((tok, grd))
         ]
 
-    from_outer = {0: send_outer(0, outer), 2: send_outer(2, inner), 1: send_outer(1, outer)}
-
-    def send_y(d, lo):
-        src = rows(16 * lo, 16, 16)
-        dst = rows({1: 2, 3: 1, 2: 3}[d] * 32 + 16 * lo, 16, 16)
-        return push(buf.at[:, z, first, c, src, :], buf.at[:, z, first, c, dst, :], along_y[d])
-
-    y_near = [send_y(1, x_lo), send_y(3, x_lo)]
-    y_far = [send_y(2, x_lo)]
+    from_outer = {0: send_outer(0, outer), 2: send_outer(2, inner)}
+
+    blocks = (x_lo, 1 - x_lo)
+
+    def send_y(d, b):
+        n = {1: 2, 3: 1, 2: 3}[d]
+        lo = blocks[b]
+        return push(buf.at[:, z, first, c, 0, lo], buf.at[:, z, first, c, n, lo], along_y[d])
+
+    def near(b, s, q):
+        return buf.at[:, q, s, c, 1:3, blocks[b]]
+
+    def far(b, s, q):
+        return buf.at[:, q, s, c, 3:4, blocks[b]]
+
+    core_piece = {(i, u): [] for i in range(4) for u in (0, 1)}
+
+    def to_sibling(i, u, which, b):
+        ref = which(b, half(u), quarter[i])
+        core_piece[i, u].append(push(ref, ref, sibling))
+
+    from_z, swaps = {}, {}
+
+    def spread(which, b, u):
+        ref = which(b, half(u), z)
+        from_z[which, b, u] = push(ref, ref, along_z[1]), push(ref, ref, along_z[3])
+        to_sibling(0, u, which, b)
+
+    def swap(which, b):
+        ref = which(b, first, z)
+        swaps[which, b] = push(ref, ref, across)
+
+    y_near, y_far = [send_y(1, 0), send_y(3, 0)], [send_y(2, 0)]
+    arrived(*y_near)
+    spread(near, 0, 0)
+    arrived(*y_far)
+    spread(far, 0, 0)
     arrived(*from_outer[0])
-    y_near += [send_y(1, 1 - x_lo), send_y(3, 1 - x_lo)]
-    y_far += [send_y(2, 1 - x_lo)]
+    y_near, y_far = [send_y(1, 1), send_y(3, 1)], [send_y(2, 1)]
+    swap(near, 0)
+    swap(far, 0)
 
     def send_w(h):
-        start, size = PARTS[h]
+        start, size = COME[h]
         return [
             push(
                 wt.at[:, rows(Q * mod4(y + d) + start, size, 16), :],
@@ -164,57 +193,44 @@
             for d in (1, 3, 2)
         ]
 
-    from_w = [send_w(h) for h in range(len(PARTS))]
+    from_w = [send_w(h) for h in range(len(COME))]
 
     def outer_to_sibling(i):
-        ref = buf.at[:, quarter[i], :, c, outer_rows, :]
+        ref = buf.at[:, quarter[i], :, c, 0, 1 - x_lo]
         return push(ref, ref, sibling)
 
     core_outer = [outer_to_sibling(0)]
 
-    def near(s, q):
-        return buf.at[:, q, s, c, 32:96, :]
-
-    def far(s, q):
-        return buf.at[:, q, s, c, 96:128, :]
-
-    core_piece = {(i, u): [] for i in range(4) for u in (0, 1)}
-
-    def to_sibling(i, u, which):
-        ref = which(half(u), quarter[i])
-        core_piece[i, u].append(push(ref, ref, sibling))
-
-    from_z = {}
-
-    def spread(which, u):
-        ref = which(half(u), z)
-        from_z[which, u] = push(ref, ref, along_z[1]), push(ref, ref, along_z[3])
-        to_sibling(0, u, which)
-
     arrived(*y_near)
-    swap_near = push(near(first, z), near(first, z), across)
-    spread(near, 0)
+    swap(near, 1)
+    spread(near, 1, 0)
     arrived(*y_far)
-    swap_far = push(far(first, z), far(first, z), across)
-    spread(far, 0)
+    swap(far, 1)
+    spread(far, 1, 0)
+    from_outer[1] = send_outer(1, outer)
     from_outer[3] = send_outer(3, outer)
-    arrived(swap_near)
-    spread(near, 1)
+    for b in (0, 1):
+        for which in (near, far):
+            arrived(swaps[which, b])
+            spread(which, b, 1)
+    for i in (1, 2):
+        arrived(*from_outer[i])
+        core_outer.append(outer_to_sibling(i))
 
     onward = []
 
-    def relay(which, u):
-        up, down = from_z[which, u]
+    def relay(which, b, u):
+        up, down = from_z[which, b, u]
         arrived(up)
         if u == 0:
-            ref = which(half(u), quarter[2])
-            onward.append((push(ref, ref, along_z[1]), which, u))
-        to_sibling(2, u, which)
+            ref = which(b, half(u), quarter[2])
+            onward.append((push(ref, ref, along_z[1]), which, b, u))
+        to_sibling(2, u, which, b)
         arrived(down)
         if u == 1:
-            ref = which(half(u), quarter[1])
-            onward.append((push(ref, ref, along_z[3]), which, u))
-        to_sibling(1, u, which)
+            ref = which(b, half(u), quarter[1])
+            onward.append((push(ref, ref, along_z[3]), which, b, u))
+        to_sibling(1, u, which, b)
 
     exchange = {}
 
@@ -273,10 +289,10 @@
         for u in (0, 1):
             pair = pair + dot_nn(
                 part[i, u, 0:2, hidden, :].reshape(2 * size, 256),
-                buf[0, q, half(u), :, :, at].reshape(256, B),
+                buf[0, q, half(u), :, :, :, :, at].reshape(256, B),
             )
             third = third + dot_nn(
-                part[i, u, 2, hidden, :], buf[1, q, half(u), :, :, at].reshape(256, B)
+                part[i, u, 2, hidden, :], buf[1, q, half(u), :, :, :, :, at].reshape(256, B)
             )
         return pair.reshape(2, size, B), third
 
@@ -299,7 +315,7 @@
     from_dw, own_dw = {}, []
 
     def last_weight_grads(i, span):
-        if span == H0:
+        if span == D0:
             for copies in from_w:
                 for copy in copies:
                     left(copy)
@@ -412,78 +428,80 @@
                 )
 
     whole, one, two = (0, 1), (0,), (1,)
-    arrived(swap_far)
-    spread(far, 1)
-    relay(near, 0)
-    arrived(*core_outer, *core_piece[0, 0], *core_piece[0, 1])
+    for b in (0, 1):
+        relay(near, b, 0)
+        relay(far, b, 0)
+    arrived(core_outer[0], *core_piece[0, 0], *core_piece[0, 1])
     own_w.wait()
     arrived(*from_w[0])
     forward(0, whole, H0)
-    relay(far, 0)
+    arrived(*core_outer[1:], *core_piece[1, 0], *core_piece[2, 0])
+    forward(1, one, H0)
+    relay(near, 0, 1)
+    relay(far, 0, 1)
     arrived(*from_w[1])
     forward(0, whole, H1)
-    for i in (1, 2):
-        arrived(*from_outer[i])
-        core_outer.append(outer_to_sibling(i))
-    arrived(*core_outer[1:], *core_piece[1, 0], *core_piece[2, 0])
-    forward(1, one, H01)
-    forward(2, one, H01)
+    forward(2, one, D0)
     activate(0, whole, H0)
-    relay(near, 1)
-    activate(0, whole, H1)
+    relay(near, 1, 1)
+    relay(far, 1, 1)
+    activate(1, one, H0)
     arrived(*from_w[2])
     forward(0, whole, H2)
-    forward(1, one, H2)
-    forward(2, one, H2)
-    relay(far, 1)
+    forward(1, one, H12)
     arrived(*core_piece[1, 1])
     forward(1, two, ALL)
-    activate(1, one, H01)
-    activate(2, one, H01)
     arrived(*core_piece[2, 1])
-    forward(2, two, H0)
+    forward(2, two, D0)
+    activate(0, whole, H1)
+    weight_grads(0, H01)
+    activate(2, one, D0)
     activate(0, whole, H2)
     token_grads(0, whole)
-    weight_grads(0, ALL)
+    weight_grads(0, H2)
     along_y_grads()
-    activate(1, one, H2)
+    activate(1, one, H12)
     token_grads(1, one)
-    activate(2, one, H2)
-    token_grads(2, one)
-    along_z_grads(1, one)
-    for copy, which, u in onward:
+    for copy, which, b, u in onward:
         arrived(copy)
-        to_sibling(3, u, which)
+        to_sibling(3, u, which, b)
     arrived(*from_outer[3])
     core_outer.append(outer_to_sibling(3))
-    along_z_grads(2, one)
+    along_z_grads(1, one)
+    arrived(core_outer[3], *core_piece[3, 0], *core_piece[3, 1])
+    forward(3, whole, D0)
     activate(1, two, ALL)
     token_grads(1, two)
-    arrived(core_outer[3], *core_piece[3, 0], *core_piece[3, 1])
-    forward(3, whole, H0)
-    forward(2, two, H12)
+    forward(2, one, D12)
+    weight_grads(1, ALL)
     along_z_grads(1, two)
-    forward(3, whole, H1)
-    weight_grads(1, ALL)
-    activate(2, two, H0)
-    weight_grads(2, H0)
+    activate(2, two, D0)
+    weight_grads(2, D0)
     then_along_z()
-    forward(3, one, H2)
-    forward(3, two, H2)
-    activate(3, whole, H0)
-    last_weight_grads(3, H0)
-    activate(2, two, H12)
+    forward(3, one, D12)
+    activate(3, whole, D0)
+    last_weight_grads(3, D0)
+    forward(2, two, D1)
+    forward(3, two, D1)
+    activate(2, one, D12)
+    token_grads(2, one)
+    forward(2, two, D2)
+    forward(3, two, D2)
+    along_z_grads(2, one)
+    activate(3, one, D12)
+    token_grads(3, one)
+    activate(2, two, D1)
+    along_z_grads(3, one)
+    weight_grads(2, D1)
+    activate(3, two, D1)
+    last_weight_grads(3, D1)
+    activate(2, two, D2)
     token_grads(2, two)
-    weight_grads(2, H12)
+    activate(3, two, D2)
+    core_last = last_token_grads()
     along_z_grads(2, two)
-    activate(3, whole, H1)
-    last_weight_grads(3, H1)
-    activate(3, one, H2)
-    token_grads(3, one)
-    activate(3, two, H2)
-    core_last = last_token_grads()
-    last_weight_grads(3, H2)
-    along_z_grads(3, one)
+    weight_grads(2, D2)
+    last_weight_grads(3, D2)
     last_along_z(core_last)
 
     def landed(ref, sem):
@@ -492,30 +510,39 @@
             device_id=along_z[1], device_id_type=MESH,
         ).wait_recv()
 
-    for d in (1, 2, 3):
-        for i, u in ((1, 0), (1, 1), (2, 0), (2, 1), (3, 0)):
+    def land(i, u):
+        for d in (1, 2, 3):
             q = mod4(z - d + offs[i])
             landed(zr.at[q, u, d - 1], zsem.at[q, u, d - 1])
+
     keep = block_rows(z - y)
     from_x, from_yg = [], {}
 
-    def over_x(k, d):
+    def over_x(u, at, own):
+        for i in range(4):
+            q = quarter[i]
+            terms = [zr[q, u, e - 1, :, at] for e in (1, 2, 3) if (offs[i] + e) % 4]
+            if i:
+                terms.append(dxs[i, u, c, keep, at])
+            if own:
+                terms.append(zy[3 - offs[i], u] if i else zs[0, u])
+            total = sum(term.astype(F32) for term in terms).astype(BF16)
+            ys[0, q, half(u), :, at] = total[0:16]
+            ys[1, q, half(u), :, at] = total[16:32]
+
+    def first_over_x():
+        for d in (1, 3, 2, 0):
+            over_x(0, cols(mod4(y + d), B), d == 0)
+        return push(ys.at[1 - x_hi, :, half(0)], xr.at[:, half(0)], across)
+
+    def then_over_x(k, d):
         at = cols(mod4(y + d), B)
         for e in (1, 2, 3):
             landed(zr.at[mod4(z - e + 2), 1, e - 1, :, at], lastsem.at[k, e - 1])
-
-        for i in range(4):
-            q = quarter[i]
-            for u in (0, 1):
-                terms = [zr[q, u, e - 1, :, at] for e in (1, 2, 3) if (offs[i] + e) % 4]
-                if i:
-                    terms.append(dxs[i, u, c, keep, at])
-                if d == 0:
-                    terms.append(zy[3 - offs[i], u] if i else zs[0, u])
-                total = sum(term.astype(F32) for term in terms).astype(BF16)
-                ys[0, q, half(u), :, at] = total[0:16]
-                ys[1, q, half(u), :, at] = total[16:32]
-        from_x.append(push(ys.at[1 - x_hi, :, :, :, at], xr.at[:, :, :, at], across))
+        over_x(1, at, d == 0)
+        from_x.append(
+            push(ys.at[1 - x_hi, :, half(1), :, at], xr.at[:, half(1), :, at], across)
+        )
 
     def over_y(k, d):
         at = cols(mod4(y + d), B)
@@ -527,15 +554,21 @@
             from_yg[d] = push(ys.at[x_hi, :, :, :, at], yr.at[d - 1], along_y[d])
 
     order = (1, 3, 2, 0)
+    for i in (1, 2, 3):
+        land(i, 0)
     arrived(*from_zy.values())
-    over_x(0, order[0])
+    from_first = first_over_x()
+    land(1, 1)
+    land(2, 1)
+    then_over_x(0, order[0])
+    arrived(from_first)
     for k in (1, 2, 3):
-        over_x(k, order[k])
+        then_over_x(k, order[k])
         over_y(k - 1, order[k - 1])
     over_y(3, order[3])
     for copy in own_dw:
         copy.wait()
-    for span in PARTS:
+    for span in GO:
         arrived(*from_dw[span])
     total = ys[x_hi, :, :, :, cols(y, B)].astype(F32)
     for d in (1, 3, 2):
@@ -546,8 +579,8 @@
 
 
 def finish(back, down, dgate, dup, ddown):
-    dgate[...] = back[0].T.astype(F32)
-    dup[...] = back[1].T.astype(F32)
+    dgate[...] = back[0].astype(F32).T
+    dup[...] = back[1].astype(F32).T
     ddown[...] = down[...].astype(F32)
 
 
@@ -567,7 +600,7 @@
             pl.BlockSpec(memory_space=pltpu.VMEM),
         ),
         scratch_shapes=[
-            pltpu.VMEM((2, 4, 2, 2, 128, DH), BF16),
+            pltpu.VMEM((2, 4, 2, 2, 4, 2, 16, DH), BF16),
             pltpu.VMEM((2, B, 4 * Q), BF16),
             pltpu.VMEM((3, 4 * Q, B), BF16),
             pltpu.VMEM((3, Q, DH), BF16),
@@ -583,8 +616,8 @@
             pltpu.VMEM((3, 2, 128, B), BF16),
             pltpu.VMEM((4, 2, 32, B), BF16),
             pltpu.VMEM((3, 2, 32, B), BF16),
-            pltpu.SemaphoreType.DMA((160,)),
-            pltpu.SemaphoreType.DMA((160,)),
+            pltpu.SemaphoreType.DMA((224,)),
+            pltpu.SemaphoreType.DMA((224,)),
             pltpu.SemaphoreType.DMA((24,)),
             pltpu.SemaphoreType.DMA((4, 2, 3)),
             pltpu.SemaphoreType.DMA((4, 3)),
@@ -599,21 +632,22 @@
     )
     grads = pl.pallas_call(
         finish,
-        grid=(7,),
+        grid=(2,),
         out_shape=(
             jax.ShapeDtypeStruct((B, 4 * Q), F32),
             jax.ShapeDtypeStruct((B, 4 * Q), F32),
             jax.ShapeDtypeStruct((4 * Q, B), F32),
         ),
         in_specs=[
-            pl.BlockSpec((2, 128, B), lambda n: (0, n, 0)),
-            pl.BlockSpec((128, B), lambda n: (n, 0)),
+            pl.BlockSpec((2, 4 * Q, B // 2), lambda n: (0, 0, n)),
+            pl.BlockSpec((2 * Q, B), lambda n: (n, 0)),
         ],
         out_specs=(
-            pl.BlockSpec((B, 128), lambda n: (0, n)),
-            pl.BlockSpec((B, 128), lambda n: (0, n)),
-            pl.BlockSpec((128, B), lambda n: (n, 0)),
+            pl.BlockSpec((B // 2, 4 * Q), lambda n: (n, 0)),
+            pl.BlockSpec((B // 2, 4 * Q), lambda n: (n, 0)),
+            pl.BlockSpec((2 * Q, B), lambda n: (n, 0)),
         ),
+        compiler_params=pltpu.CompilerParams(vmem_limit_bytes=40 * 2**20),
         cost_estimate=pl.CostEstimate(flops=0, bytes_accessed=2**23, transcendentals=0),
     )(back, ddown)
     return (dx, *grads)

time: 146 us -> 141 us (0.966)
  Pallas kernels: 144 us -> 137 us
  local copies, waits for them, and re-layouts: 0.66 us -> 3.33 us
    pallas_call x1, Pallas kernels: 138 us -> 134 us  [local(): pl.pallas_call(kernel, out_shape=(jax.ShapeDtypeStruct((2, 4 * Q, B), BF1...]
    pallas_call x1, Pallas kernels: 6.27 us -> 2.8 us  [local(): pl.pallas_call(finish, grid=(2,), out_shape=(jax.ShapeDtypeStruct((B, 4 *...]
    unnamed x3 -> x7, local copies, waits for them, and re-layouts: 0.66 us -> 3.33 us
where the time goes in v7:
time: 141 us
  Pallas kernels  137 us (97%)
  local copies, waits for them, and re-layouts  3.33 us (2%)
    pallas_call x1, Pallas kernels, local(): pl.pallas_call(kernel, out_shape=(jax.ShapeDtypeStruct((2, 4 * Q, B), BF1...  134 us
    unnamed x7, local copies, waits for them, and re-layouts  3.33 us

profile of v7, /device:TPU:0, one launch (start us, length us, event | category | flops | bytes accessed | tf_op | source)
XLA Modules:
  0.0 140.9 jit_solution(14178069723204735781)
XLA Ops:
  0.6 134.2 %shard_map.84 = (bf16[2,896,512]{2,1,0:T(8,128)(2,1)}, bf16[896,512]{1,0:T(8,128)(2,1)}, bf16[128,512]{1,0:T(8,128)(2,1)}) custom-call(bf16[2,4,2,16,4096]{4,3,2,1,0:T(8,128)(2,1)} %bitcast.2, bf16[2,4,2,16,4096]{4,3,2,1,0:T(8,128)(2,1)} %bitcast.3, bf16[512,896]{1,0:T(8,128)(2,1)} %gate_w.1, bf16[512,896]{1,0:T(8,128)(2,1)} %up_w.1, bf16[896,512]{1,0:T(8,128)(2,1)} %down_w.1), custom_call_target="tpu_custom_call" | custom-call | flops 17179869184 | bytes 16777216 | tf_op jit(solution)/shard_map/pallas_call | solution.py:589
  134.8 0.0 copy-start
  134.8 1.5 %copy-done = bf16[2,896,512]{2,1,0:T(8,128)(2,1)S(1)} copy-done((bf16[2,896,512]{2,1,0:T(8,128)(2,1)S(1)}, bf16[2,896,512]{2,1,0:T(8,128)(2,1)}, u32[]{:S(2)}) %copy-start) | copy-done | bytes 1835032
  136.3 0.0 copy-start.1
  136.3 1.2 copy-done.1
  137.5 0.0 copy-start.2
  137.5 2.8 %shard_map.85 = (f32[512,896]{1,0:T(8,128)}, f32[512,896]{1,0:T(8,128)}, f32[896,512]{1,0:T(8,128)}) custom-call(bf16[2,896,512]{2,1,0:T(8,128)(2,1)S(1)} %copy-done, bf16[896,512]{1,0:T(8,128)(2,1)S(1)} %copy-done.1), custom_call_target="tpu_custom_call" | custom-call | bytes 8388608 | tf_op jit(solution)/shard_map/pallas_call | solution.py:633
  140.3 0.0 copy-done.2
  140.3 0.7 copy.10
Async XLA Ops:
  134.8 1.5 %copy-start = (bf16[2,896,512]{2,1,0:T(8,128)(2,1)S(1)}, bf16[2,896,512]{2,1,0:T(8,128)(2,1)}, u32[]{:S(2)}) copy-start(bf16[2,896,512]{2,1,0:T(8,128)(2,1)} %get-tuple-element.11.back) | copy-start | bytes 5505028
  136.3 1.2 copy-start.1
  137.5 2.8 %copy-start.2 = (bf16[128,512]{1,0:T(8,128)(2,1)S(1)}, bf16[128,512]{1,0:T(8,128)(2,1)}, u32[]{:S(2)}) copy-start(bf16[128,512]{1,0:T(8,128)(2,1)} %get-tuple-element.20) | copy-start | bytes 393220

commit v8 on v7

--- a/solution.py
+++ b/solution.py
@@ -15,9 +15,9 @@
 DH = 2048
 B = 512
 CHUNK = 512
-H0, H1, H2 = COME = ((0, 80), (80, 80), (160, 64))
+H0, H1, H2 = COME = ((0, 64), (64, 80), (144, 80))
 D0, D1, D2 = GO = ((0, 96), (96, 64), (160, 64))
-H01, H12, D12, ALL = (0, 160), (80, 144), (96, 128), (0, Q)
+H01, H12, REST0, D12, ALL = (0, 144), (64, 160), (64, 32), (96, 128), (0, Q)
 
 
 def dot_nt(left, right):
@@ -213,9 +213,8 @@
         for which in (near, far):
             arrived(swaps[which, b])
             spread(which, b, 1)
-    for i in (1, 2):
-        arrived(*from_outer[i])
-        core_outer.append(outer_to_sibling(i))
+    arrived(*from_outer[2])
+    core_outer.append(outer_to_sibling(2))
 
     onward = []
 
@@ -409,7 +408,7 @@
     def last_token_grads():
         core_last = {}
         deltas = turned(3, 1)
-        for d in (1, 3, 2, 0):
+        for d in (2, 1, 3, 0):
             n = mod4(y + d)
             token_terms(3, 1, n, deltas)
             at = cols(n, B)
@@ -417,7 +416,7 @@
         return core_last
 
     def last_along_z(core_last):
-        for k, d in enumerate((1, 3, 2, 0)):
+        for k, d in enumerate((2, 1, 3, 0)):
             at = cols(mod4(y + d), B)
             arrived(core_last[d])
             add_core(3, 1, at)
@@ -435,13 +434,17 @@
     own_w.wait()
     arrived(*from_w[0])
     forward(0, whole, H0)
-    arrived(*core_outer[1:], *core_piece[1, 0], *core_piece[2, 0])
+    arrived(core_outer[1], *core_piece[2, 0])
+    forward(2, one, H0)
+    arrived(*from_outer[1])
+    core_outer.append(outer_to_sibling(1))
+    arrived(core_outer[2], *core_piece[1, 0])
     forward(1, one, H0)
     relay(near, 0, 1)
     relay(far, 0, 1)
     arrived(*from_w[1])
     forward(0, whole, H1)
-    forward(2, one, D0)
+    forward(2, one, REST0)
     activate(0, whole, H0)
     relay(near, 1, 1)
     relay(far, 1, 1)
@@ -455,7 +458,8 @@
     forward(2, two, D0)
     activate(0, whole, H1)
     weight_grads(0, H01)
-    activate(2, one, D0)
+    activate(2, one, H0)
+    activate(2, one, REST0)
     activate(0, whole, H2)
     token_grads(0, whole)
     weight_grads(0, H2)
@@ -498,8 +502,8 @@
     activate(2, two, D2)
     token_grads(2, two)
     activate(3, two, D2)
+    along_z_grads(2, two)
     core_last = last_token_grads()
-    along_z_grads(2, two)
     weight_grads(2, D2)
     last_weight_grads(3, D2)
     last_along_z(core_last)
@@ -553,7 +557,7 @@
         if d:
             from_yg[d] = push(ys.at[x_hi, :, :, :, at], yr.at[d - 1], along_y[d])
 
-    order = (1, 3, 2, 0)
+    order = (2, 1, 3, 0)
     for i in (1, 2, 3):
         land(i, 0)
     arrived(*from_zy.values())
@@ -571,7 +575,7 @@
     for span in GO:
         arrived(*from_dw[span])
     total = ys[x_hi, :, :, :, cols(y, B)].astype(F32)
-    for d in (1, 3, 2):
+    for d in (2, 1, 3):
         arrived(from_yg[d])
         total = total + yr[d - 1].astype(F32)
     dx[...] = total.astype(BF16).reshape(128, B)
@@ -647,7 +651,7 @@
             pl.BlockSpec((B // 2, 4 * Q), lambda n: (n, 0)),
             pl.BlockSpec((2 * Q, B), lambda n: (n, 0)),
         ),
-        compiler_params=pltpu.CompilerParams(vmem_limit_bytes=40 * 2**20),
+        compiler_params=pltpu.CompilerParams(vmem_limit_bytes=62 * 2**20),
         cost_estimate=pl.CostEstimate(flops=0, bytes_accessed=2**23, transcendentals=0),
     )(back, ddown)
     return (dx, *grads)

time: 141 us -> 137 us (0.972)
  local copies, waits for them, and re-layouts: 3.33 us -> 0.66 us
    unnamed x7 -> x3, local copies, waits for them, and re-layouts: 3.33 us -> 0.66 us
    pallas_call x1, Pallas kernels: 134 us -> 132 us  [local(): pl.pallas_call(kernel, out_shape=(jax.ShapeDtypeStruct((2, 4 * Q, B), BF1...]
where the time goes in v8:
time: 137 us
  Pallas kernels  136 us (99%)
    pallas_call x1, Pallas kernels, local(): pl.pallas_call(kernel, out_shape=(jax.ShapeDtypeStruct((2, 4 * Q, B), BF1...  132 us
    pallas_call x1, Pallas kernels, local(): pl.pallas_call(finish, grid=(2,), out_shape=(jax.ShapeDtypeStruct((B, 4 *...  3.99 us

profile of v8, /device:TPU:0, one launch (start us, length us, event | category | flops | bytes accessed | tf_op | source)
XLA Modules:
  0.0 137.1 jit_solution(8386496198191803991)
XLA Ops:
  0.6 131.8 %shard_map.84 = (bf16[2,896,512]{2,1,0:T(8,128)(2,1)}, bf16[896,512]{1,0:T(8,128)(2,1)}, bf16[128,512]{1,0:T(8,128)(2,1)}) custom-call(bf16[2,4,2,16,4096]{4,3,2,1,0:T(8,128)(2,1)} %bitcast.2, bf16[2,4,2,16,4096]{4,3,2,1,0:T(8,128)(2,1)} %bitcast.3, bf16[512,896]{1,0:T(8,128)(2,1)} %gate_w.1, bf16[512,896]{1,0:T(8,128)(2,1)} %up_w.1, bf16[896,512]{1,0:T(8,128)(2,1)} %down_w.1), custom_call_target="tpu_custom_call" | custom-call | flops 17179869184 | bytes 16777216 | tf_op jit(solution)/shard_map/pallas_call | solution.py:593
  132.5 0.0 copy-start
  132.5 4.0 %shard_map.85 = (f32[512,896]{1,0:T(8,128)}, f32[512,896]{1,0:T(8,128)}, f32[896,512]{1,0:T(8,128)}) custom-call(bf16[2,896,512]{2,1,0:T(8,128)(2,1)} %get-tuple-element.11.back, bf16[896,512]{1,0:T(8,128)(2,1)} %get-tuple-element.12.down), custom_call_target="tpu_custom_call" | custom-call | bytes 8388608 | tf_op jit(solution)/shard_map/pallas_call | solution.py:637
  136.5 0.0 copy-done
  136.5 0.7 copy.10
Async XLA Ops:
  132.5 4.0 %copy-start = (bf16[128,512]{1,0:T(8,128)(2,1)S(1)}, bf16[128,512]{1,0:T(8,128)(2,1)}, u32[]{:S(2)}) copy-start(bf16[128,512]{1,0:T(8,128)(2,1)} %get-tuple-element.20) | copy-start | bytes 393220

commit v9 on v8

--- a/solution.py
+++ b/solution.py
@@ -17,7 +17,7 @@
 CHUNK = 512
 H0, H1, H2 = COME = ((0, 64), (64, 80), (144, 80))
 D0, D1, D2 = GO = ((0, 96), (96, 64), (160, 64))
-H01, H12, REST0, D12, ALL = (0, 144), (64, 160), (64, 32), (96, 128), (0, Q)
+H01, D12, ALL = (0, 144), (96, 128), (0, Q)
 
 
 def dot_nt(left, right):
@@ -427,13 +427,15 @@
                 )
 
     whole, one, two = (0, 1), (0,), (1,)
+    own_w.wait()
+    arrived(core_outer[0], *core_piece[0, 0])
+    arrived(*from_w[0])
+    forward(0, one, H0)
+    arrived(*core_piece[0, 1])
+    forward(0, two, H0)
     for b in (0, 1):
         relay(near, b, 0)
         relay(far, b, 0)
-    arrived(core_outer[0], *core_piece[0, 0], *core_piece[0, 1])
-    own_w.wait()
-    arrived(*from_w[0])
-    forward(0, whole, H0)
     arrived(core_outer[1], *core_piece[2, 0])
     forward(2, one, H0)
     arrived(*from_outer[1])
@@ -444,27 +446,30 @@
     relay(far, 0, 1)
     arrived(*from_w[1])
     forward(0, whole, H1)
-    forward(2, one, REST0)
-    activate(0, whole, H0)
+    forward(2, one, H1)
+    forward(1, one, H1)
+    activate(0, one, H0)
+    activate(0, two, H0)
     relay(near, 1, 1)
     relay(far, 1, 1)
+    activate(2, one, H0)
     activate(1, one, H0)
     arrived(*from_w[2])
     forward(0, whole, H2)
-    forward(1, one, H12)
+    forward(1, one, H2)
     arrived(*core_piece[1, 1])
     forward(1, two, ALL)
     arrived(*core_piece[2, 1])
     forward(2, two, D0)
     activate(0, whole, H1)
     weight_grads(0, H01)
-    activate(2, one, H0)
-    activate(2, one, REST0)
+    activate(2, one, H1)
+    activate(1, one, H1)
     activate(0, whole, H2)
     token_grads(0, whole)
     weight_grads(0, H2)
     along_y_grads()
-    activate(1, one, H12)
+    activate(1, one, H2)
     token_grads(1, one)
     for copy, which, b, u in onward:
         arrived(copy)
@@ -476,7 +481,7 @@
     forward(3, whole, D0)
     activate(1, two, ALL)
     token_grads(1, two)
-    forward(2, one, D12)
+    forward(2, one, H2)
     weight_grads(1, ALL)
     along_z_grads(1, two)
     activate(2, two, D0)
@@ -486,12 +491,12 @@
     activate(3, whole, D0)
     last_weight_grads(3, D0)
     forward(2, two, D1)
+    activate(2, one, H2)
+    token_grads(2, one)
     forward(3, two, D1)
-    activate(2, one, D12)
-    token_grads(2, one)
+    along_z_grads(2, one)
     forward(2, two, D2)
     forward(3, two, D2)
-    along_z_grads(2, one)
     activate(3, one, D12)
     token_grads(3, one)
     activate(2, two, D1)
@@ -582,7 +587,8 @@
     left(*sent)
 
 
-def finish(back, down, dgate, dup, ddown):
+def finish(back, down, tokens, dgate, dup, ddown, dx):
+    dx[...] = tokens[...]
     dgate[...] = back[0].astype(F32).T
     dup[...] = back[1].astype(F32).T
     ddown[...] = down[...].astype(F32)
@@ -641,20 +647,23 @@
             jax.ShapeDtypeStruct((B, 4 * Q), F32),
             jax.ShapeDtypeStruct((B, 4 * Q), F32),
             jax.ShapeDtypeStruct((4 * Q, B), F32),
+            jax.ShapeDtypeStruct((128, B), BF16),
         ),
         in_specs=[
             pl.BlockSpec((2, 4 * Q, B // 2), lambda n: (0, 0, n)),
             pl.BlockSpec((2 * Q, B), lambda n: (n, 0)),
+            pl.BlockSpec((64, B), lambda n: (n, 0)),
         ],
         out_specs=(
             pl.BlockSpec((B // 2, 4 * Q), lambda n: (n, 0)),
             pl.BlockSpec((B // 2, 4 * Q), lambda n: (n, 0)),
             pl.BlockSpec((2 * Q, B), lambda n: (n, 0)),
+            pl.BlockSpec((64, B), lambda n: (n, 0)),
         ),
         compiler_params=pltpu.CompilerParams(vmem_limit_bytes=62 * 2**20),
         cost_estimate=pl.CostEstimate(flops=0, bytes_accessed=2**23, transcendentals=0),
-    )(back, ddown)
-    return (dx, *grads)
+    )(back, ddown, dx)
+    return (grads[3], *grads[:3])
 
 
 def solution(mesh):

time: 137 us -> 136 us (level)
  no operation moved by 1% of the time
where the time goes in v9:
time: 136 us; the launch traced here: 135 us
  Pallas kernels  135 us (99%)
    pallas_call x1, Pallas kernels, local(): pl.pallas_call(kernel, out_shape=(jax.ShapeDtypeStruct((2, 4 * Q, B), BF1...  131 us
    pallas_call x1, Pallas kernels, local(): pl.pallas_call(finish, grid=(2,), out_shape=(jax.ShapeDtypeStruct((B, 4 *...  4.03 us

profile of v9, /device:TPU:0, one launch (start us, length us, event | category | flops | bytes accessed | tf_op | source)
XLA Modules:
  0.0 135.3 jit_solution(16210187779368039494)
XLA Ops:
  0.6 130.6 %shard_map.84 = (bf16[2,896,512]{2,1,0:T(8,128)(2,1)}, bf16[896,512]{1,0:T(8,128)(2,1)}, bf16[128,512]{1,0:T(8,128)(2,1)}) custom-call(bf16[2,4,2,16,4096]{4,3,2,1,0:T(8,128)(2,1)} %bitcast.2, bf16[2,4,2,16,4096]{4,3,2,1,0:T(8,128)(2,1)} %bitcast.3, bf16[512,896]{1,0:T(8,128)(2,1)} %gate_w.1, bf16[512,896]{1,0:T(8,128)(2,1)} %up_w.1, bf16[896,512]{1,0:T(8,128)(2,1)} %down_w.1), custom_call_target="tpu_custom_call" | custom-call | flops 17179869184 | bytes 16777216 | tf_op jit(solution)/shard_map/pallas_call | solution.py:599
  131.3 4.0 %shard_map.85 = (f32[512,896]{1,0:T(8,128)}, f32[512,896]{1,0:T(8,128)}, f32[896,512]{1,0:T(8,128)}, bf16[128,512]{1,0:T(8,128)(2,1)}) custom-call(bf16[2,896,512]{2,1,0:T(8,128)(2,1)} %get-tuple-element.11.back, bf16[896,512]{1,0:T(8,128)(2,1)} %get-tuple-element.12.down, bf16[128,512]{1,0:T(8,128)(2,1)} %get-tuple-element.13.tokens), custom_call_target="tpu_custom_call" | custom-call | bytes 8388608 | tf_op jit(solution)/shard_map/pallas_call | solution.py:643

commit v10 on v9

--- a/solution.py
+++ b/solution.py
@@ -120,6 +120,50 @@
         for a, src in enumerate((tok, grd))
     ]
     own_raw = [bring(gate_w, raw.at[0]), bring(up_w, raw.at[1]), bring(down_w, wt.at[2])]
+    pl.semaphore_wait(barrier, len(partners))
+
+    def send_outer(i, target):
+        q = quarter[i]
+        return [
+            push(src.at[c, q, :, :, theirs], buf.at[a, q, :, c, 0, x_lo], target)
+            for a, src in enumerate((tok, grd))
+        ]
+
+    from_outer = {0: send_outer(0, outer), 2: send_outer(2, inner)}
+
+    blocks = (x_lo, 1 - x_lo)
+
+    def send_y(d, b):
+        n = {1: 2, 3: 1, 2: 3}[d]
+        lo = blocks[b]
+        return push(buf.at[:, z, first, c, 0, lo], buf.at[:, z, first, c, n, lo], along_y[d])
+
+    def near(b, s, q):
+        return buf.at[:, q, s, c, 1:3, blocks[b]]
+
+    def far(b, s, q):
+        return buf.at[:, q, s, c, 3:4, blocks[b]]
+
+    core_piece = {(i, u): [] for i in range(4) for u in (0, 1)}
+
+    def to_sibling(i, u, which, b):
+        ref = which(b, half(u), quarter[i])
+        core_piece[i, u].append(push(ref, ref, sibling))
+
+    from_z, swaps = {}, {}
+
+    def spread(which, b, u):
+        ref = which(b, half(u), z)
+        from_z[which, b, u] = push(ref, ref, along_z[1]), push(ref, ref, along_z[3])
+        to_sibling(0, u, which, b)
+
+    def swap(which, b):
+        ref = which(b, first, z)
+        swaps[which, b] = push(ref, ref, across)
+
+    for copy in own_tok:
+        copy.wait()
+    y_near, y_far = [send_y(1, 0), send_y(3, 0)], [send_y(2, 0)]
     for copy in own_raw:
         copy.wait()
     for m in (0, 1):
@@ -129,50 +173,6 @@
 
         lax.fori_loop(0, 7, turn, 0)
     own_w = bring(wt.at[:, rows(Q * y, Q), :], wbuf.at[:, :, cols(y, B)])
-    for copy in own_tok:
-        copy.wait()
-    pl.semaphore_wait(barrier, len(partners))
-
-    def send_outer(i, target):
-        q = quarter[i]
-        return [
-            push(src.at[c, q, :, :, theirs], buf.at[a, q, :, c, 0, x_lo], target)
-            for a, src in enumerate((tok, grd))
-        ]
-
-    from_outer = {0: send_outer(0, outer), 2: send_outer(2, inner)}
-
-    blocks = (x_lo, 1 - x_lo)
-
-    def send_y(d, b):
-        n = {1: 2, 3: 1, 2: 3}[d]
-        lo = blocks[b]
-        return push(buf.at[:, z, first, c, 0, lo], buf.at[:, z, first, c, n, lo], along_y[d])
-
-    def near(b, s, q):
-        return buf.at[:, q, s, c, 1:3, blocks[b]]
-
-    def far(b, s, q):
-        return buf.at[:, q, s, c, 3:4, blocks[b]]
-
-    core_piece = {(i, u): [] for i in range(4) for u in (0, 1)}
-
-    def to_sibling(i, u, which, b):
-        ref = which(b, half(u), quarter[i])
-        core_piece[i, u].append(push(ref, ref, sibling))
-
-    from_z, swaps = {}, {}
-
-    def spread(which, b, u):
-        ref = which(b, half(u), z)
-        from_z[which, b, u] = push(ref, ref, along_z[1]), push(ref, ref, along_z[3])
-        to_sibling(0, u, which, b)
-
-    def swap(which, b):
-        ref = which(b, first, z)
-        swaps[which, b] = push(ref, ref, across)
-
-    y_near, y_far = [send_y(1, 0), send_y(3, 0)], [send_y(2, 0)]
     arrived(*y_near)
     spread(near, 0, 0)
     arrived(*y_far)
@@ -482,8 +482,8 @@
     activate(1, two, ALL)
     token_grads(1, two)
     forward(2, one, H2)
+    along_z_grads(1, two)
     weight_grads(1, ALL)
-    along_z_grads(1, two)
     activate(2, two, D0)
     weight_grads(2, D0)
     then_along_z()

time: 136 us -> 133 us (0.978)
  Pallas kernels: 135 us -> 132 us
    pallas_call x1, Pallas kernels: 131 us -> 128 us  [local(): pl.pallas_call(kernel, out_shape=(jax.ShapeDtypeStruct((2, 4 * Q, B), BF1...]
where the time goes in v10:
time: 133 us; the launch traced here: 132 us
  Pallas kernels  132 us (99%)
    pallas_call x1, Pallas kernels, local(): pl.pallas_call(kernel, out_shape=(jax.ShapeDtypeStruct((2, 4 * Q, B), BF1...  128 us
    pallas_call x1, Pallas kernels, local(): pl.pallas_call(finish, grid=(2,), out_shape=(jax.ShapeDtypeStruct((B, 4 *...  4.03 us

profile of v10, /device:TPU:0, one launch (start us, length us, event | category | flops | bytes accessed | tf_op | source)
XLA Modules:
  0.0 132.2 jit_solution(6966267672912335570)
XLA Ops:
  0.6 127.6 %shard_map.84 = (bf16[2,896,512]{2,1,0:T(8,128)(2,1)}, bf16[896,512]{1,0:T(8,128)(2,1)}, bf16[128,512]{1,0:T(8,128)(2,1)}) custom-call(bf16[2,4,2,16,4096]{4,3,2,1,0:T(8,128)(2,1)} %bitcast.2, bf16[2,4,2,16,4096]{4,3,2,1,0:T(8,128)(2,1)} %bitcast.3, bf16[512,896]{1,0:T(8,128)(2,1)} %gate_w.1, bf16[512,896]{1,0:T(8,128)(2,1)} %up_w.1, bf16[896,512]{1,0:T(8,128)(2,1)} %down_w.1), custom_call_target="tpu_custom_call" | custom-call | flops 17179869184 | bytes 16777216 | tf_op jit(solution)/shard_map/pallas_call | solution.py:599
  128.2 4.0 %shard_map.85 = (f32[512,896]{1,0:T(8,128)}, f32[512,896]{1,0:T(8,128)}, f32[896,512]{1,0:T(8,128)}, bf16[128,512]{1,0:T(8,128)(2,1)}) custom-call(bf16[2,896,512]{2,1,0:T(8,128)(2,1)} %get-tuple-element.11.back, bf16[896,512]{1,0:T(8,128)(2,1)} %get-tuple-element.12.down, bf16[128,512]{1,0:T(8,128)(2,1)} %get-tuple-element.13.tokens), custom_call_target="tpu_custom_call" | custom-call | bytes 8388608 | tf_op jit(solution)/shard_map/pallas_call | solution.py:643

commit v11 on v10

--- a/solution.py
+++ b/solution.py
@@ -129,7 +129,14 @@
             for a, src in enumerate((tok, grd))
         ]
 
-    from_outer = {0: send_outer(0, outer), 2: send_outer(2, inner)}
+    from_outer = {
+        0: [
+            push(src.at[c, z, s, :, theirs], buf.at[a, z, s, c, 0, x_lo], outer)
+            for s in (second, first)
+            for a, src in enumerate((tok, grd))
+        ]
+    }
+    from_outer[2] = send_outer(2, inner)
 
     blocks = (x_lo, 1 - x_lo)
 
@@ -177,7 +184,7 @@
     spread(near, 0, 0)
     arrived(*y_far)
     spread(far, 0, 0)
-    arrived(*from_outer[0])
+    arrived(*from_outer[0][:2])
     y_near, y_far = [send_y(1, 1), send_y(3, 1)], [send_y(2, 1)]
     swap(near, 0)
     swap(far, 0)
@@ -199,6 +206,7 @@
         ref = buf.at[:, quarter[i], :, c, 0, 1 - x_lo]
         return push(ref, ref, sibling)
 
+    arrived(*from_outer[0][2:])
     core_outer = [outer_to_sibling(0)]
 
     arrived(*y_near)

time: 133 us -> 133 us (level)
  no operation moved by 1% of the time
where the time goes in v11:
time: 133 us
  Pallas kernels  132 us (99%)
    pallas_call x1, Pallas kernels, local(): pl.pallas_call(kernel, out_shape=(jax.ShapeDtypeStruct((2, 4 * Q, B), BF1...  128 us
    pallas_call x1, Pallas kernels, local(): pl.pallas_call(finish, grid=(2,), out_shape=(jax.ShapeDtypeStruct((B, 4 *...  4.03 us

profile of v11, /device:TPU:0, one launch (start us, length us, event | category | flops | bytes accessed | tf_op | source)
XLA Modules:
  0.0 132.8 jit_solution(16238541924483107993)
XLA Ops:
  0.6 128.1 %shard_map.84 = (bf16[2,896,512]{2,1,0:T(8,128)(2,1)}, bf16[896,512]{1,0:T(8,128)(2,1)}, bf16[128,512]{1,0:T(8,128)(2,1)}) custom-call(bf16[2,4,2,16,4096]{4,3,2,1,0:T(8,128)(2,1)} %bitcast.2, bf16[2,4,2,16,4096]{4,3,2,1,0:T(8,128)(2,1)} %bitcast.3, bf16[512,896]{1,0:T(8,128)(2,1)} %gate_w.1, bf16[512,896]{1,0:T(8,128)(2,1)} %up_w.1, bf16[896,512]{1,0:T(8,128)(2,1)} %down_w.1), custom_call_target="tpu_custom_call" | custom-call | flops 17179869184 | bytes 16777216 | tf_op jit(solution)/shard_map/pallas_call | solution.py:607
  128.7 4.0 %shard_map.85 = (f32[512,896]{1,0:T(8,128)}, f32[512,896]{1,0:T(8,128)}, f32[896,512]{1,0:T(8,128)}, bf16[128,512]{1,0:T(8,128)(2,1)}) custom-call(bf16[2,896,512]{2,1,0:T(8,128)(2,1)} %get-tuple-element.11.back, bf16[896,512]{1,0:T(8,128)(2,1)} %get-tuple-element.12.down, bf16[128,512]{1,0:T(8,128)(2,1)} %get-tuple-element.13.tokens), custom_call_target="tpu_custom_call" | custom-call | bytes 8388608 | tf_op jit(solution)/shard_map/pallas_call | solution.py:651
